TPU v7x, 32 devices: a whole 2x2x4 slice. The times are simulated.
32 devices in a mesh: tx: 2 (over y), ty: 4 (over z), gz: 4 (over x, core).
Axes of the slice: x: 2, y: 2, z: 4, core: 2. Of those that a mesh axis runs over, the one named last changes fastest.
Arguments:
- tracer_in: float32 [100, 256, 256], P('gz', 'ty', 'tx'), may hold values from -6 to 6
- coef_h: float32 [3, 256, 256], P(None, 'ty', 'tx'), may hold values from 0.05 to 0.2
- coef_v: float32 [3, 100], replicated, may hold values from 0.3 to 1
- wet_levels: int32 [256, 256], P('ty', 'tx'), may hold values from 0 to 100
- column_inv: float32 [100, 100], replicated, may hold values from -0.1 to 1
- sec_cell: int32 [2048], P(('tx', 'ty')), may hold values from 0 to 8191
- sec_gate: int32 [2048], P(('tx', 'ty')), may hold values from 0 to 63
- sec_weight: float32 [2048], P(('tx', 'ty')), may hold values from -6 to 6
Outputs:
- tracer_out: float32 [100, 256, 256], P('gz', 'ty', 'tx')
- gate_flux: float32 [64, 100], P(('tx', 'ty'), 'gz')
Inputs may be any that keep to these rules, and one draw needn't show every extreme that they name: `sec_cell`: index of a cell within the tile of the slot.
All inputs are finite; a program needn't handle non-finite values.
Results may differ from a plain program's by a relative error of at most 0.00015.
Values sent between devices are 32-bit elements; how exact they have to be, the bound alone decides.
A program may use at most 64 MiB of HBM per device.

v0:
```python
import jax
import jax.numpy as jnp
from jax import lax
from jax.sharding import PartitionSpec as P

NSUB = 3
STEPS = 2
G_DEV = 8


def extended(block, sides, width):
    for axis, dim in sides:
        count = lax.axis_size(axis)
        forward = [(i, i + 1) for i in range(count - 1)]
        backward = [(target, source) for source, target in forward]
        low = lax.ppermute(
            lax.slice_in_dim(block, block.shape[dim] - width, None, axis=dim), axis, forward
        )
        high = lax.ppermute(lax.slice_in_dim(block, 0, width, axis=dim), axis, backward)
        block = jnp.concatenate([low, block, high], axis=dim)
    return block


def diffuse(padded, coef_h, coef_v, wet):
    centre = padded[:, 1:-1, 1:-1]
    coef_x = coef_h[0][None] * coef_v[0][:, None, None]
    coef_y = coef_h[1][None] * coef_v[1][:, None, None]
    coef_s = coef_h[2][None] * coef_v[2][:, None, None]
    along_x = padded[:, 1:-1, 2:] - 2.0 * centre + padded[:, 1:-1, :-2]
    along_y = padded[:, 2:, 1:-1] - 2.0 * centre + padded[:, :-2, 1:-1]
    cross = padded[:, 2:, 2:] - padded[:, 2:, :-2] - padded[:, :-2, 2:] + padded[:, :-2, :-2]
    return wet * (centre + coef_x * along_x + coef_y * along_y + 0.25 * coef_s * cross)


def vertical(field, column_inv, wet):
    levels = column_inv.shape[0]
    flat = field.reshape(levels, -1)
    solved = jnp.dot(column_inv.T, flat, precision=lax.Precision.HIGHEST)
    return wet * solved.reshape(field.shape)


def per_device(tracer_in, coef_h, coef_v, wet_levels, column_inv, sec_cell, sec_gate, sec_weight):
    depth_count = lax.axis_size("gz")
    depth_index = lax.axis_index("gz")
    local_levels, rows, width = tracer_in.shape
    levels = local_levels * depth_count
    col_rows = rows // depth_count
    slot_count = sec_cell.shape[0]
    level_ids = depth_index * local_levels + jnp.arange(local_levels, dtype=jnp.int32)
    wet_depth = (level_ids[:, None, None] < wet_levels[None]).astype(jnp.float32)
    coef_depth = lax.dynamic_slice_in_dim(coef_v, depth_index * local_levels, local_levels, 1)
    row_start = depth_index * col_rows
    wet_rows = lax.dynamic_slice_in_dim(wet_levels, row_start, col_rows, 0)
    wet_column = (jnp.arange(levels, dtype=jnp.int32)[:, None, None] < wet_rows[None]).astype(
        jnp.float32
    )
    adjoint = wet_depth * tracer_in
    slot_sum = jnp.zeros((local_levels, slot_count), jnp.float32)
    for step_index in range(STEPS):
        for substep in range(NSUB):
            padded = extended(adjoint, (("tx", 2), ("ty", 1)), 1)
            adjoint = diffuse(padded, coef_h, coef_depth, wet_depth)
        columns = lax.all_to_all(adjoint, "gz", split_axis=1, concat_axis=0, tiled=True)
        columns = vertical(columns, column_inv, wet_column)
        adjoint = lax.all_to_all(columns, "gz", split_axis=0, concat_axis=1, tiled=True)
        values = adjoint.reshape(local_levels, rows * width)[:, sec_cell]
        slot_sum = slot_sum + values * sec_weight[None, :]
    gate_ids = jnp.arange(G_DEV * lax.axis_size(("tx", "ty")), dtype=jnp.int32)
    onehot = (sec_gate[:, None] == gate_ids[None, :]).astype(jnp.float32)
    gate_flux = lax.psum_scatter(
        jnp.dot(slot_sum, onehot, precision=lax.Precision.HIGHEST).T,
        ("tx", "ty"),
        scatter_dimension=0,
        tiled=True,
    )
    return (adjoint, gate_flux)


def solution(mesh):
    in_specs = (
        P("gz", "ty", "tx"),
        P(None, "ty", "tx"),
        P(),
        P("ty", "tx"),
        P(),
        P(("tx", "ty")),
        P(("tx", "ty")),
        P(("tx", "ty")),
    )
    out_specs = (P("gz", "ty", "tx"), P(("tx", "ty"), "gz"))
    return jax.shard_map(
        per_device, mesh=mesh, in_specs=in_specs, out_specs=out_specs, check_vma=False
    )
```

profile of v0, /device:TPU:0, one launch (start us, length us, event | category | flops | bytes accessed | tf_op | source)
XLA Modules:
  0.0 241.7 jit_solution(2131519805706094154)
XLA Ops:
  4.3 4.9 %collective-permute-start.1 = (f32[25,64,1]{1,0,2:T(8,128)S(1)}, f32[25,64,1]{1,0,2:T(8,128)S(1)}, u32[]{:S(2)}, u32[]{:S(2)}) collective-permute-start(f32[25,64,1]{1,0,2:T(8,128)S(1)} %copy.78), channel_id=1, source_target_pairs={{0,16},{1,17},{2,18},{3,19},{4,20},{5,21},{6,22},{7,23},{8,24},{9,... | collective-permute-start | bytes 19208 | tf_op jit(solution)/shard_map/ppermute | solution.py:16
  12.8 5.2 %collective-permute-start.3 = (f32[25,1,130]{2,1,0:T(1,128)S(1)}, f32[25,1,130]{2,1,0:T(1,128)S(1)}, u32[]{:S(2)}, u32[]{:S(2)}) collective-permute-start(f32[25,1,130]{2,1,0:T(1,128)S(1)} %get-tuple-element.25), channel_id=1, source_target_pairs={{0,4},{4,8},{8,12},{1,5},{5,9},{9,13},{2,6},{6,10},{10,14},{3,7},{... | collective-permute-start | bytes 39008 | tf_op jit(solution)/shard_map/ppermute | solution.py:16
  23.5 4.2 %collective-permute-start.5 = (f32[25,64,1]{1,0,2:T(8,128)S(1)}, f32[25,64,1]{1,0,2:T(8,128)S(1)}, u32[]{:S(2)}, u32[]{:S(2)}) collective-permute-start(f32[25,64,1]{1,0,2:T(8,128)S(1)} %copy.84), channel_id=1, source_target_pairs={{0,16},{1,17},{2,18},{3,19},{4,20},{5,21},{6,22},{7,23},{8,24},{9,... | collective-permute-start | bytes 19208 | tf_op jit(solution)/shard_map/ppermute | solution.py:16
  29.7 4.0 %collective-permute-done.4 = f32[25,64,1]{1,0,2:T(8,128)S(1)} collective-permute-done((f32[25,64,1]{1,0,2:T(8,128)S(1)}, f32[25,64,1]{1,0,2:T(8,128)S(1)}, u32[]{:S(2)}, u32[]{:S(2)}) %collective-permute-start.4) | collective-permute-done | bytes 6432 | tf_op jit(solution)/shard_map/ppermute | solution.py:19
  35.6 4.8 %collective-permute-start.7 = (f32[25,1,130]{2,1,0:T(1,128)S(1)}, f32[25,1,130]{2,1,0:T(1,128)S(1)}, u32[]{:S(2)}, u32[]{:S(2)}) collective-permute-start(f32[25,1,130]{2,1,0:T(1,128)S(1)} %get-tuple-element.21), channel_id=1, source_target_pairs={{0,4},{4,8},{8,12},{1,5},{5,9},{9,13},{2,6},{6,10},{10,14},{3,7},{... | collective-permute-start | bytes 39008 | tf_op jit(solution)/shard_map/ppermute | solution.py:16
  49.5 4.0 %collective-permute-done.8 = f32[25,64,1]{1,0,2:T(8,128)S(1)} collective-permute-done((f32[25,64,1]{1,0,2:T(8,128)S(1)}, f32[25,64,1]{1,0,2:T(8,128)S(1)}, u32[]{:S(2)}, u32[]{:S(2)}) %collective-permute-start.8) | collective-permute-done | bytes 6432 | tf_op jit(solution)/shard_map/ppermute | solution.py:19
  55.3 5.0 %collective-permute-start.11 = (f32[25,1,130]{2,1,0:T(1,128)S(1)}, f32[25,1,130]{2,1,0:T(1,128)S(1)}, u32[]{:S(2)}, u32[]{:S(2)}) collective-permute-start(f32[25,1,130]{2,1,0:T(1,128)S(1)} %get-tuple-element.17), channel_id=1, source_target_pairs={{0,4},{4,8},{8,12},{1,5},{5,9},{9,13},{2,6},{6,10},{10,14},{3,7},{... | collective-permute-start | bytes 39008 | tf_op jit(solution)/shard_map/ppermute | solution.py:16
  66.4 3.5 %all-to-all-start = ((f32[25,64,128]{2,0,1:T(8,128)}), f32[25,64,128]{2,0,1:T(8,128)S(1)}, u32[]{:S(2)}, u32[]{:S(2)}) async-start(f32[25,64,128]{2,0,1:T(8,128)} %copy.94), calls=%async_computation | async-start | bytes 2097152 | tf_op jit(solution)/shard_map/all_to_all | solution.py:63
  69.9 14.4 %all-to-all-done = f32[25,64,128]{2,0,1:T(8,128)S(1)} async-done(((f32[25,64,128]{2,0,1:T(8,128)}), f32[25,64,128]{2,0,1:T(8,128)S(1)}, u32[]{:S(2)}, u32[]{:S(2)}) %all-to-all-start) | async-done | bytes 819232 | tf_op jit(solution)/shard_map/all_to_all | solution.py:63
  86.3 14.4 %all_to_all.66 = f32[100,16,128]{2,1,0:T(8,128)S(1)} all-to-all(f32[100,16,128]{2,1,0:T(8,128)S(1)} %slice_select_fusion.1), channel_id=1, replica_groups=mesh['tx'=2,'ty'=4,'gz'=4] {'gz'}, dimensions={0} | all-to-all | bytes 1638400 | tf_op jit(solution)/shard_map/all_to_all | solution.py:65
  106.0 4.0 %collective-permute-done.12 = f32[25,64,1]{1,0,2:T(8,128)S(1)} collective-permute-done((f32[25,64,1]{1,0,2:T(8,128)S(1)}, f32[25,64,1]{1,0,2:T(8,128)S(1)}, u32[]{:S(2)}, u32[]{:S(2)}) %collective-permute-start.12) | collective-permute-done | bytes 6432 | tf_op jit(solution)/shard_map/ppermute | solution.py:19
  111.9 4.8 %collective-permute-start.15 = (f32[25,1,130]{2,1,0:T(1,128)S(1)}, f32[25,1,130]{2,1,0:T(1,128)S(1)}, u32[]{:S(2)}, u32[]{:S(2)}) collective-permute-start(f32[25,1,130]{2,1,0:T(1,128)S(1)} %get-tuple-element.13), channel_id=1, source_target_pairs={{0,4},{4,8},{8,12},{1,5},{5,9},{9,13},{2,6},{6,10},{10,14},{3,7},{... | collective-permute-start | bytes 39008 | tf_op jit(solution)/shard_map/ppermute | solution.py:16
  125.8 4.0 %collective-permute-done.16 = f32[25,64,1]{1,0,2:T(8,128)S(1)} collective-permute-done((f32[25,64,1]{1,0,2:T(8,128)S(1)}, f32[25,64,1]{1,0,2:T(8,128)S(1)}, u32[]{:S(2)}, u32[]{:S(2)}) %collective-permute-start.16) | collective-permute-done | bytes 6432 | tf_op jit(solution)/shard_map/ppermute | solution.py:19
  131.7 5.1 %collective-permute-start.19 = (f32[25,1,130]{2,1,0:T(1,128)S(1)}, f32[25,1,130]{2,1,0:T(1,128)S(1)}, u32[]{:S(2)}, u32[]{:S(2)}) collective-permute-start(f32[25,1,130]{2,1,0:T(1,128)S(1)} %get-tuple-element.9), channel_id=1, source_target_pairs={{0,4},{4,8},{8,12},{1,5},{5,9},{9,13},{2,6},{6,10},{10,14},{3,7},{... | collective-permute-start | bytes 39008 | tf_op jit(solution)/shard_map/ppermute | solution.py:16
  145.6 4.0 %collective-permute-done.20 = f32[25,64,1]{1,0,2:T(8,128)S(1)} collective-permute-done((f32[25,64,1]{1,0,2:T(8,128)S(1)}, f32[25,64,1]{1,0,2:T(8,128)S(1)}, u32[]{:S(2)}, u32[]{:S(2)}) %collective-permute-start.20) | collective-permute-done | bytes 6432 | tf_op jit(solution)/shard_map/ppermute | solution.py:19
  151.4 4.8 %collective-permute-start.23 = (f32[25,1,130]{2,1,0:T(1,128)S(1)}, f32[25,1,130]{2,1,0:T(1,128)S(1)}, u32[]{:S(2)}, u32[]{:S(2)}) collective-permute-start(f32[25,1,130]{2,1,0:T(1,128)S(1)} %get-tuple-element.5), channel_id=1, source_target_pairs={{0,4},{4,8},{8,12},{1,5},{5,9},{9,13},{2,6},{6,10},{10,14},{3,7},{... | collective-permute-start | bytes 39008 | tf_op jit(solution)/shard_map/ppermute | solution.py:16
  161.5 16.9 %all_to_all.67 = f32[25,64,128]{2,0,1:T(8,128)S(1)} all-to-all(f32[25,64,128]{2,0,1:T(8,128)S(1)} %copy.115), channel_id=1, replica_groups=mesh['tx'=2,'ty'=4,'gz'=4] {'gz'}, dimensions={1} | all-to-all | bytes 1638400 | tf_op jit(solution)/shard_map/all_to_all | solution.py:63
  181.2 3.5 %all-to-all-start.3 = ((f32[100,16,128]{2,1,0:T(8,128)}), f32[100,16,128]{2,1,0:T(8,128)S(1)}, u32[]{:S(2)}, u32[]{:S(2)}) async-start(f32[100,16,128]{2,1,0:T(8,128)} %slice_select_fusion), calls=%async_computation.3 | async-start | bytes 1638400 | tf_op jit(solution)/shard_map/all_to_all | solution.py:65
  186.0 2.7 %copy.119 = f32[25,4,16,128]{0,3,2,1:T(8,128)} copy(f32[25,4,16,128]{3,2,0,1:T(8,128)S(1)} %bitcast.54) | data formatting | bytes 1638400 | tf_op jit(solution)/shard_map/all_to_all | solution.py:65
  188.7 2.9 %gather_fusion = f32[256,25]{1,0:T(8,128)S(1)} fusion(f32[25,8192]{0,1:T(8,128)} %bitcast.58, s32[1024]{0:T(1024)S(1)} %pad_clamp_fusion), kind=kCustom, calls=%fused_computation | custom fusion | bytes 52224 | tf_op jit(solution)/shard_map/gather | solution.py:66
  191.7 5.1 %all-to-all-done.3 = f32[100,16,128]{2,1,0:T(8,128)S(1)} async-done(((f32[100,16,128]{2,1,0:T(8,128)}), f32[100,16,128]{2,1,0:T(8,128)S(1)}, u32[]{:S(2)}, u32[]{:S(2)}) %all-to-all-start.3) | async-done | bytes 819232 | tf_op jit(solution)/shard_map/all_to_all | solution.py:65
  197.7 2.7 %copy.117 = f32[4,25,16,128]{1,3,2,0:T(8,128)} copy(f32[4,25,16,128]{3,2,1,0:T(8,128)S(1)} %bitcast.56) | data formatting | bytes 1638400 | tf_op jit(solution)/shard_map/all_to_all | solution.py:65
  200.4 2.9 %gather_fusion.1 = f32[256,25]{1,0:T(8,128)S(1)} fusion(f32[25,8192]{0,1:T(8,128)} %bitcast.57, s32[1024]{0:T(1024)S(1)} %pad_clamp_fusion), kind=kCustom, calls=%fused_computation.1 | custom fusion | bytes 52224 | tf_op jit(solution)/shard_map/gather | solution.py:66
  203.7 37.4 %all-reduce = f32[64,25]{1,0:T(8,128)S(1)} all-reduce(f32[64,25]{1,0:T(8,128)S(1)} %fusion.36), channel_id=2, replica_groups=mesh['tx'=2,'ty'=4,'gz'=4] {'tx','ty'}, use_global_device_ids=true, to_apply=%region_0.0.clone | all-reduce | flops 1600 | bytes 12800
  (130 shorter events, 74.4 us)
Async XLA Ops:
  2.6 8.3 %collective-permute-start = (f32[25,64,1]{1,0,2:T(8,128)S(1)}, f32[25,64,1]{1,0,2:T(8,128)S(1)}, u32[]{:S(2)}, u32[]{:S(2)}) collective-permute-start(f32[25,64,1]{1,0,2:T(8,128)S(1)} %copy.76), channel_id=1, source_target_pairs={{16,0},{17,1},{18,2},{19,3},{20,4},{21,5},{22,6},{23,7},{24,8},{25... | collective-permute-start | bytes 19208 | tf_op jit(solution)/shard_map/ppermute | solution.py:19
  4.3 6.3 %collective-permute-start.1 = (f32[25,64,1]{1,0,2:T(8,128)S(1)}, f32[25,64,1]{1,0,2:T(8,128)S(1)}, u32[]{:S(2)}, u32[]{:S(2)}) collective-permute-start(f32[25,64,1]{1,0,2:T(8,128)S(1)} %copy.78), channel_id=1, source_target_pairs={{0,16},{1,17},{2,18},{3,19},{4,20},{5,21},{6,22},{7,23},{8,24},{9,... | collective-permute-start | bytes 19208 | tf_op jit(solution)/shard_map/ppermute | solution.py:16
  11.5 6.6 %collective-permute-start.2 = (f32[25,1,130]{2,1,0:T(1,128)S(1)}, f32[25,1,130]{2,1,0:T(1,128)S(1)}, u32[]{:S(2)}, u32[]{:S(2)}) collective-permute-start(f32[25,1,130]{2,1,0:T(1,128)S(1)} %get-tuple-element.24), channel_id=1, source_target_pairs={{4,0},{8,4},{12,8},{5,1},{9,5},{13,9},{6,2},{10,6},{14,10},{7,3},{... | collective-permute-start | bytes 39008 | tf_op jit(solution)/shard_map/ppermute | solution.py:19
  12.8 6.8 %collective-permute-start.3 = (f32[25,1,130]{2,1,0:T(1,128)S(1)}, f32[25,1,130]{2,1,0:T(1,128)S(1)}, u32[]{:S(2)}, u32[]{:S(2)}) collective-permute-start(f32[25,1,130]{2,1,0:T(1,128)S(1)} %get-tuple-element.25), channel_id=1, source_target_pairs={{0,4},{4,8},{8,12},{1,5},{5,9},{9,13},{2,6},{6,10},{10,14},{3,7},{... | collective-permute-start | bytes 39008 | tf_op jit(solution)/shard_map/ppermute | solution.py:16
  23.5 5.9 %collective-permute-start.5 = (f32[25,64,1]{1,0,2:T(8,128)S(1)}, f32[25,64,1]{1,0,2:T(8,128)S(1)}, u32[]{:S(2)}, u32[]{:S(2)}) collective-permute-start(f32[25,64,1]{1,0,2:T(8,128)S(1)} %copy.84), channel_id=1, source_target_pairs={{0,16},{1,17},{2,18},{3,19},{4,20},{5,21},{6,22},{7,23},{8,24},{9,... | collective-permute-start | bytes 19208 | tf_op jit(solution)/shard_map/ppermute | solution.py:16
  28.1 5.6 %collective-permute-start.4 = (f32[25,64,1]{1,0,2:T(8,128)S(1)}, f32[25,64,1]{1,0,2:T(8,128)S(1)}, u32[]{:S(2)}, u32[]{:S(2)}) collective-permute-start(f32[25,64,1]{1,0,2:T(8,128)S(1)} %copy.82), channel_id=1, source_target_pairs={{16,0},{17,1},{18,2},{19,3},{20,4},{21,5},{22,6},{23,7},{24,8},{25... | collective-permute-start | bytes 19208 | tf_op jit(solution)/shard_map/ppermute | solution.py:19
  34.3 6.2 %collective-permute-start.6 = (f32[25,1,130]{2,1,0:T(1,128)S(1)}, f32[25,1,130]{2,1,0:T(1,128)S(1)}, u32[]{:S(2)}, u32[]{:S(2)}) collective-permute-start(f32[25,1,130]{2,1,0:T(1,128)S(1)} %get-tuple-element.20), channel_id=1, source_target_pairs={{4,0},{8,4},{12,8},{5,1},{9,5},{13,9},{6,2},{10,6},{14,10},{7,3},{... | collective-permute-start | bytes 39008 | tf_op jit(solution)/shard_map/ppermute | solution.py:19
  35.6 6.4 %collective-permute-start.7 = (f32[25,1,130]{2,1,0:T(1,128)S(1)}, f32[25,1,130]{2,1,0:T(1,128)S(1)}, u32[]{:S(2)}, u32[]{:S(2)}) collective-permute-start(f32[25,1,130]{2,1,0:T(1,128)S(1)} %get-tuple-element.21), channel_id=1, source_target_pairs={{0,4},{4,8},{8,12},{1,5},{5,9},{9,13},{2,6},{6,10},{10,14},{3,7},{... | collective-permute-start | bytes 39008 | tf_op jit(solution)/shard_map/ppermute | solution.py:16
  45.8 3.3 %collective-permute-start.9 = (f32[25,64,1]{1,0,2:T(8,128)S(1)}, f32[25,64,1]{1,0,2:T(8,128)S(1)}, u32[]{:S(2)}, u32[]{:S(2)}) collective-permute-start(f32[25,64,1]{1,0,2:T(8,128)S(1)} %copy.90), channel_id=1, source_target_pairs={{0,16},{1,17},{2,18},{3,19},{4,20},{5,21},{6,22},{7,23},{8,24},{9,... | collective-permute-start | bytes 19208 | tf_op jit(solution)/shard_map/ppermute | solution.py:16
  47.8 5.6 %collective-permute-start.8 = (f32[25,64,1]{1,0,2:T(8,128)S(1)}, f32[25,64,1]{1,0,2:T(8,128)S(1)}, u32[]{:S(2)}, u32[]{:S(2)}) collective-permute-start(f32[25,64,1]{1,0,2:T(8,128)S(1)} %copy.88), channel_id=1, source_target_pairs={{16,0},{17,1},{18,2},{19,3},{20,4},{21,5},{22,6},{23,7},{24,8},{25... | collective-permute-start | bytes 19208 | tf_op jit(solution)/shard_map/ppermute | solution.py:19
  54.0 6.3 %collective-permute-start.10 = (f32[25,1,130]{2,1,0:T(1,128)S(1)}, f32[25,1,130]{2,1,0:T(1,128)S(1)}, u32[]{:S(2)}, u32[]{:S(2)}) collective-permute-start(f32[25,1,130]{2,1,0:T(1,128)S(1)} %get-tuple-element.16), channel_id=1, source_target_pairs={{4,0},{8,4},{12,8},{5,1},{9,5},{13,9},{6,2},{10,6},{14,10},{7,3},{... | collective-permute-start | bytes 39008 | tf_op jit(solution)/shard_map/ppermute | solution.py:19
  55.3 6.4 %collective-permute-start.11 = (f32[25,1,130]{2,1,0:T(1,128)S(1)}, f32[25,1,130]{2,1,0:T(1,128)S(1)}, u32[]{:S(2)}, u32[]{:S(2)}) collective-permute-start(f32[25,1,130]{2,1,0:T(1,128)S(1)} %get-tuple-element.17), channel_id=1, source_target_pairs={{0,4},{4,8},{8,12},{1,5},{5,9},{9,13},{2,6},{6,10},{10,14},{3,7},{... | collective-permute-start | bytes 39008 | tf_op jit(solution)/shard_map/ppermute | solution.py:16
  66.4 18.0 %all-to-all-start = ((f32[25,64,128]{2,0,1:T(8,128)}), f32[25,64,128]{2,0,1:T(8,128)S(1)}, u32[]{:S(2)}, u32[]{:S(2)}) async-start(f32[25,64,128]{2,0,1:T(8,128)} %copy.94), calls=%async_computation | async-start | bytes 2097152 | tf_op jit(solution)/shard_map/all_to_all | solution.py:63
  102.4 3.3 %collective-permute-start.13 = (f32[25,64,1]{1,0,2:T(8,128)S(1)}, f32[25,64,1]{1,0,2:T(8,128)S(1)}, u32[]{:S(2)}, u32[]{:S(2)}) collective-permute-start(f32[25,64,1]{1,0,2:T(8,128)S(1)} %copy.99), channel_id=1, source_target_pairs={{0,16},{1,17},{2,18},{3,19},{4,20},{5,21},{6,22},{7,23},{8,24},{9,... | collective-permute-start | bytes 19208 | tf_op jit(solution)/shard_map/ppermute | solution.py:16
  104.4 5.6 %collective-permute-start.12 = (f32[25,64,1]{1,0,2:T(8,128)S(1)}, f32[25,64,1]{1,0,2:T(8,128)S(1)}, u32[]{:S(2)}, u32[]{:S(2)}) collective-permute-start(f32[25,64,1]{1,0,2:T(8,128)S(1)} %copy.97), channel_id=1, source_target_pairs={{16,0},{17,1},{18,2},{19,3},{20,4},{21,5},{22,6},{23,7},{24,8},{25... | collective-permute-start | bytes 19208 | tf_op jit(solution)/shard_map/ppermute | solution.py:19
  110.6 6.1 %collective-permute-start.14 = (f32[25,1,130]{2,1,0:T(1,128)S(1)}, f32[25,1,130]{2,1,0:T(1,128)S(1)}, u32[]{:S(2)}, u32[]{:S(2)}) collective-permute-start(f32[25,1,130]{2,1,0:T(1,128)S(1)} %get-tuple-element.12), channel_id=1, source_target_pairs={{4,0},{8,4},{12,8},{5,1},{9,5},{13,9},{6,2},{10,6},{14,10},{7,3},{... | collective-permute-start | bytes 39008 | tf_op jit(solution)/shard_map/ppermute | solution.py:19
  111.9 6.4 %collective-permute-start.15 = (f32[25,1,130]{2,1,0:T(1,128)S(1)}, f32[25,1,130]{2,1,0:T(1,128)S(1)}, u32[]{:S(2)}, u32[]{:S(2)}) collective-permute-start(f32[25,1,130]{2,1,0:T(1,128)S(1)} %get-tuple-element.13), channel_id=1, source_target_pairs={{0,4},{4,8},{8,12},{1,5},{5,9},{9,13},{2,6},{6,10},{10,14},{3,7},{... | collective-permute-start | bytes 39008 | tf_op jit(solution)/shard_map/ppermute | solution.py:16
  124.2 5.6 %collective-permute-start.16 = (f32[25,64,1]{1,0,2:T(8,128)S(1)}, f32[25,64,1]{1,0,2:T(8,128)S(1)}, u32[]{:S(2)}, u32[]{:S(2)}) collective-permute-start(f32[25,64,1]{1,0,2:T(8,128)S(1)} %copy.103), channel_id=1, source_target_pairs={{16,0},{17,1},{18,2},{19,3},{20,4},{21,5},{22,6},{23,7},{24,8},{25... | collective-permute-start | bytes 19208 | tf_op jit(solution)/shard_map/ppermute | solution.py:19
  130.4 6.4 %collective-permute-start.18 = (f32[25,1,130]{2,1,0:T(1,128)S(1)}, f32[25,1,130]{2,1,0:T(1,128)S(1)}, u32[]{:S(2)}, u32[]{:S(2)}) collective-permute-start(f32[25,1,130]{2,1,0:T(1,128)S(1)} %get-tuple-element.8), channel_id=1, source_target_pairs={{4,0},{8,4},{12,8},{5,1},{9,5},{13,9},{6,2},{10,6},{14,10},{7,3},{... | collective-permute-start | bytes 39008 | tf_op jit(solution)/shard_map/ppermute | solution.py:19
  131.7 6.4 %collective-permute-start.19 = (f32[25,1,130]{2,1,0:T(1,128)S(1)}, f32[25,1,130]{2,1,0:T(1,128)S(1)}, u32[]{:S(2)}, u32[]{:S(2)}) collective-permute-start(f32[25,1,130]{2,1,0:T(1,128)S(1)} %get-tuple-element.9), channel_id=1, source_target_pairs={{0,4},{4,8},{8,12},{1,5},{5,9},{9,13},{2,6},{6,10},{10,14},{3,7},{... | collective-permute-start | bytes 39008 | tf_op jit(solution)/shard_map/ppermute | solution.py:16
  143.9 5.6 %collective-permute-start.20 = (f32[25,64,1]{1,0,2:T(8,128)S(1)}, f32[25,64,1]{1,0,2:T(8,128)S(1)}, u32[]{:S(2)}, u32[]{:S(2)}) collective-permute-start(f32[25,64,1]{1,0,2:T(8,128)S(1)} %copy.109), channel_id=1, source_target_pairs={{16,0},{17,1},{18,2},{19,3},{20,4},{21,5},{22,6},{23,7},{24,8},{25... | collective-permute-start | bytes 19208 | tf_op jit(solution)/shard_map/ppermute | solution.py:19
  150.1 6.2 %collective-permute-start.22 = (f32[25,1,130]{2,1,0:T(1,128)S(1)}, f32[25,1,130]{2,1,0:T(1,128)S(1)}, u32[]{:S(2)}, u32[]{:S(2)}) collective-permute-start(f32[25,1,130]{2,1,0:T(1,128)S(1)} %get-tuple-element.4), channel_id=1, source_target_pairs={{4,0},{8,4},{12,8},{5,1},{9,5},{13,9},{6,2},{10,6},{14,10},{7,3},{... | collective-permute-start | bytes 39008 | tf_op jit(solution)/shard_map/ppermute | solution.py:19
  151.4 6.4 %collective-permute-start.23 = (f32[25,1,130]{2,1,0:T(1,128)S(1)}, f32[25,1,130]{2,1,0:T(1,128)S(1)}, u32[]{:S(2)}, u32[]{:S(2)}) collective-permute-start(f32[25,1,130]{2,1,0:T(1,128)S(1)} %get-tuple-element.5), channel_id=1, source_target_pairs={{0,4},{4,8},{8,12},{1,5},{5,9},{9,13},{2,6},{6,10},{10,14},{3,7},{... | collective-permute-start | bytes 39008 | tf_op jit(solution)/shard_map/ppermute | solution.py:16
  181.2 15.5 %all-to-all-start.3 = ((f32[100,16,128]{2,1,0:T(8,128)}), f32[100,16,128]{2,1,0:T(8,128)S(1)}, u32[]{:S(2)}, u32[]{:S(2)}) async-start(f32[100,16,128]{2,1,0:T(8,128)} %slice_select_fusion), calls=%async_computation.3 | async-start | bytes 1638400 | tf_op jit(solution)/shard_map/all_to_all | solution.py:65
  (12 other events, 136.8 us)
where the time goes:
time: 243 us; the launch traced here: 242 us
  blocking collectives  68.7 us (28%)
  starting transfers between devices  68 us (28%)
  waiting for transfers between devices  49.3 us (20%)
  local copies, waits for them, and re-layouts  28.7 us (12%)
  other arithmetic  22.8 us (9%)
    ppermute x12, starting transfers between devices, extended(): lax.ppermute(lax.slice_in_dim(block, block.shape[dim] - width, None, axis...  45.5 us
    unnamed x1, blocking collectives  37.4 us
    ppermute x12, waiting for transfers between devices, extended(): lax.ppermute(lax.slice_in_dim(block, 0, width, axis=dim), axis, backward)  19.9 us
    all_to_all x1, blocking collectives, per_device(): lax.all_to_all(adjoint, 'gz', split_axis=1, concat_axis=0, tiled=True)  16.9 us
    ppermute x12, starting transfers between devices, extended(): lax.ppermute(lax.slice_in_dim(block, 0, width, axis=dim), axis, backward)  15.5 us
    all_to_all x1, waiting for transfers between devices, per_device(): lax.all_to_all(adjoint, 'gz', split_axis=1, concat_axis=0, tiled=True)  14.4 us
    all_to_all x1, blocking collectives, per_device(): lax.all_to_all(columns, 'gz', split_axis=0, concat_axis=1, tiled=True)  14.4 us
    mul x6, other arithmetic, diffuse(): wet * (centre + coef_x * along_x + coef_y * along_y + 0.25 * coef_s * cross)  10.6 us
  transfers between devices with their start and end apart: 26, of which 14 were waited for; matrix products, arithmetic and copies ran while one was open for 4% of the time, Pallas kernels for 0%

commit v1 on v0

v1 whole, which is shorter than its diff:
```python
import jax
import jax.numpy as jnp
from jax import lax
from jax.sharding import PartitionSpec as P

NSUB = 3
G_DEV = 8
HI = lax.Precision.HIGHEST


def extended(block, axis, dim, width):
    count = lax.axis_size(axis)
    forward = [(i, i + 1) for i in range(count - 1)]
    backward = [(target, source) for source, target in forward]
    low = lax.ppermute(
        lax.slice_in_dim(block, block.shape[dim] - width, None, axis=dim), axis, forward
    )
    high = lax.ppermute(lax.slice_in_dim(block, 0, width, axis=dim), axis, backward)
    return jnp.concatenate([low, block, high], axis=dim)


def diffuse(padded, coef_h, coef_v, wet_levels, level_ids):
    centre = padded[:, 1:-1, 1:-1]
    coef_x = coef_h[0][None] * coef_v[0][:, None, None]
    coef_y = coef_h[1][None] * coef_v[1][:, None, None]
    coef_s = coef_h[2][None] * coef_v[2][:, None, None]
    along_x = padded[:, 1:-1, 2:] - 2.0 * centre + padded[:, 1:-1, :-2]
    along_y = padded[:, 2:, 1:-1] - 2.0 * centre + padded[:, :-2, 1:-1]
    cross = padded[:, 2:, 2:] - padded[:, 2:, :-2] - padded[:, :-2, 2:] + padded[:, :-2, :-2]
    wet = (level_ids[:, None, None] < wet_levels[None]).astype(jnp.float32)
    return wet * (centre + coef_x * along_x + coef_y * along_y + 0.25 * coef_s * cross)


def substeps(field, coef_h, coef_v, wet_levels, level_ids):
    for ring in range(1, NSUB + 1):
        inner = coef_h[:, ring:-ring, ring:-ring]
        field = diffuse(field, inner, coef_v, wet_levels[ring:-ring, ring:-ring], level_ids)
    return field


def vertical(field, column_inv, wet_levels, level_ids):
    levels = column_inv.shape[0]
    flat = field.reshape(levels, -1)
    solved = jnp.dot(column_inv.T, flat, precision=HI).reshape(field.shape)
    wet = (level_ids[:, None, None] < wet_levels[None]).astype(jnp.float32)
    return wet * solved


def per_device(tracer_in, coef_h, coef_v, wet_levels, column_inv, sec_cell, sec_gate, sec_weight):
    depth_count = lax.axis_size("gz")
    depth_index = lax.axis_index("gz")
    tiles = lax.axis_size(("tx", "ty"))
    local_levels, rows, width = tracer_in.shape
    levels = local_levels * depth_count
    col_rows = rows // depth_count
    level_ids = depth_index * local_levels + jnp.arange(local_levels, dtype=jnp.int32)
    all_ids = jnp.arange(levels, dtype=jnp.int32)
    coef_depth = lax.dynamic_slice_in_dim(coef_v, depth_index * local_levels, local_levels, 1)
    row_start = depth_index * col_rows

    gate_ids = jnp.arange(G_DEV * tiles, dtype=jnp.int32)
    gate_hot = jnp.where(gate_ids[:, None] == sec_gate[None, :], sec_weight[None, :], 0.0)
    cells = row_start * width + jnp.arange(col_rows * width, dtype=jnp.int32)
    cell_hot = (sec_cell[:, None] == cells[None, :]).astype(jnp.float32)
    gate_cells = jnp.dot(gate_hot, cell_hot, precision=HI)

    rim = 2 * NSUB
    wet_depth = (level_ids[:, None, None] < wet_levels[None]).astype(jnp.float32)
    packed = jnp.concatenate(
        [wet_depth * tracer_in, coef_h, wet_levels[None].astype(jnp.float32)], axis=0
    )
    packed = extended(extended(packed, "tx", 2, rim), "ty", 1, rim)
    field = packed[:local_levels]
    coef_h = packed[local_levels:-1]
    wet_levels = packed[-1].astype(jnp.int32)

    field = substeps(field, coef_h, coef_depth, wet_levels, level_ids)
    tall = col_rows + 2 * NSUB
    sent = jnp.stack(
        [field[:, part * col_rows : part * col_rows + tall, :] for part in range(depth_count)]
    )
    sent = sent.reshape(depth_count, local_levels, -1)
    field = lax.all_to_all(sent, "gz", split_axis=0, concat_axis=0, tiled=True)
    field = field.reshape(levels, tall, -1)
    coef_h = lax.dynamic_slice_in_dim(coef_h, row_start + NSUB, tall, 1)[:, :, NSUB:-NSUB]
    wet_levels = lax.dynamic_slice_in_dim(wet_levels, row_start + NSUB, tall, 0)[:, NSUB:-NSUB]
    field = vertical(field, column_inv, wet_levels, all_ids)
    total = field[:, NSUB:-NSUB, NSUB:-NSUB]

    field = substeps(field, coef_h, coef_v, wet_levels, all_ids)
    field = vertical(field, column_inv, wet_levels[NSUB:-NSUB, NSUB:-NSUB], all_ids)
    total = total + field
    out = lax.all_to_all(field, "gz", split_axis=0, concat_axis=1, tiled=True)

    flux = lax.dot_general(
        gate_cells, total.reshape(levels, -1), (((1,), (1,)), ((), ())), precision=HI
    )
    flux = flux.reshape(tiles, G_DEV, depth_count, local_levels).transpose(0, 2, 1, 3)
    flux = flux.reshape(tiles * depth_count, G_DEV * local_levels)
    flux = lax.all_to_all(flux, ("tx", "ty", "gz"), split_axis=0, concat_axis=0, tiled=True)
    flux = jnp.sum(flux, axis=0).reshape(G_DEV, local_levels)
    return (out, flux)


def solution(mesh):
    in_specs = (
        P("gz", "ty", "tx"),
        P(None, "ty", "tx"),
        P(),
        P("ty", "tx"),
        P(),
        P(("tx", "ty")),
        P(("tx", "ty")),
        P(("tx", "ty")),
    )
    out_specs = (P("gz", "ty", "tx"), P(("tx", "ty"), "gz"))
    return jax.shard_map(
        per_device, mesh=mesh, in_specs=in_specs, out_specs=out_specs, check_vma=False
    )
```

time: 243 us -> 137 us (0.56)
  the two profiles are of different devices: /device:TPU:0 before, /device:TPU:1 now
where the time goes in v1:
time: 137 us; the launch traced here: 135 us
  waiting for transfers between devices  41.7 us (30%)
  local copies, waits for them, and re-layouts  30.3 us (22%)
  other arithmetic  29.2 us (21%)
  starting transfers between devices  25.1 us (18%)
  matrix products  7.82 us (6%)
    all_to_all x1, waiting for transfers between devices, per_device(): field = lax.all_to_all(sent, 'gz', split_axis=0, concat_axis=0, tiled=True)  16.2 us
    mul x6, other arithmetic, diffuse(): wet * (centre + coef_x * along_x + coef_y * along_y + 0.25 * coef_s * cross)  15.5 us
    all_to_all x1, waiting for transfers between devices, per_device(): out = lax.all_to_all(field, 'gz', split_axis=0, concat_axis=1, tiled=True)  10.4 us
    all_to_all x1, starting transfers between devices, per_device(): field = lax.all_to_all(sent, 'gz', split_axis=0, concat_axis=0, tiled=True)  7.96 us
    ppermute x2, waiting for transfers between devices, extended(): lax.ppermute(lax.slice_in_dim(block, 0, width, axis=dim), axis, backward)  7.3 us
    ppermute x2, starting transfers between devices, extended(): lax.ppermute(lax.slice_in_dim(block, block.shape[dim] - width, None, axis...  7.18 us
    slice x8, local copies, waits for them, and re-layouts, substeps(): wet_levels[ring:-ring, ring:-ring]  7.11 us
    another operation x4, local copies, waits for them, and re-layouts, per_device(): jnp.stack([field[:, part * col_rows:part * col_rows + tall, :] for part i...  6.45 us
  transfers between devices with their start and end apart: 7, of which 6 were waited for; matrix products, arithmetic and copies ran while one was open for 4% of the time, Pallas kernels for 0%

profile of v1, /device:TPU:1, one launch (start us, length us, event | category | flops | bytes accessed | tf_op | source)
XLA Modules:
  0.0 135.2 jit_solution(9009648317094486944)
XLA Ops:
  4.4 4.0 %collective-permute-start = (f32[29,64,6]{1,0,2:T(8,128)S(1)}, f32[29,64,6]{1,0,2:T(8,128)S(1)}, u32[]{:S(2)}, u32[]{:S(2)}) collective-permute-start(f32[29,64,6]{1,0,2:T(8,128)S(1)} %copy.47), channel_id=1, source_target_pairs={{0,16},{1,17},{2,18},{3,19},{4,20},{5,21},{6,22},{7,23},{8,24},{9,... | collective-permute-start | bytes 133640 | tf_op jit(solution)/shard_map/ppermute | solution.py:15
  10.6 3.6 %collective-permute-done.1 = f32[29,64,6]{1,0,2:T(8,128)S(1)} collective-permute-done((f32[29,64,6]{1,0,2:T(8,128)S(1)}, f32[29,64,6]{1,0,2:T(8,128)S(1)}, u32[]{:S(2)}, u32[]{:S(2)}) %collective-permute-start.1) | collective-permute-done | bytes 44576 | tf_op jit(solution)/shard_map/ppermute | solution.py:18
  15.6 3.2 %collective-permute-start.2 = (f32[29,6,140]{2,1,0:T(8,128)}, f32[29,6,140]{2,1,0:T(8,128)S(1)}, u32[]{:S(2)}, u32[]{:S(2)}) collective-permute-start(f32[29,6,140]{2,1,0:T(8,128)} %get-tuple-element.10), channel_id=1, source_target_pairs={{0,4},{4,8},{8,12},{1,5},{5,9},{9,13},{2,6},{6,10},{10,14},{3,7},{... | collective-permute-start | bytes 292328 | tf_op jit(solution)/shard_map/ppermute | solution.py:15
  20.2 2.0 %collective-permute-done.2 = f32[29,6,140]{2,1,0:T(8,128)S(1)} collective-permute-done((f32[29,6,140]{2,1,0:T(8,128)}, f32[29,6,140]{2,1,0:T(8,128)S(1)}, u32[]{:S(2)}, u32[]{:S(2)}) %collective-permute-start.2) | collective-permute-done | bytes 97472 | tf_op jit(solution)/shard_map/ppermute | solution.py:15
  22.2 3.7 %collective-permute-done.3 = f32[29,6,140]{2,1,0:T(8,128)S(1)} collective-permute-done((f32[29,6,140]{2,1,0:T(8,128)}, f32[29,6,140]{2,1,0:T(8,128)S(1)}, u32[]{:S(2)}, u32[]{:S(2)}) %collective-permute-start.3) | collective-permute-done | bytes 97472 | tf_op jit(solution)/shard_map/ppermute | solution.py:18
  35.6 2.6 %pad_maximum_fusion = f32[29,76,140]{2,1,0:T(8,128)S(1)} fusion(f32[29,6,140]{2,1,0:T(8,128)} %copy-done.5, f32[29,64,6]{2,1,0:T(8,128)} %copy-done.3, f32[1,64,128]{2,1,0:T(8,128)S(1)} %convert_bitcast_fusion, f32[3,64,128]{2,1,0:T(8,128)S(1)} %copy-done.8, f32[25,64,128]{2,1,0:T(8,128)S(1)} %compare_select_fusion, f32[29,64,6]{2,1,0:T(8,128)} %copy-done.1, ...), kind=kLoop, calls=%fused_computation.2 | loop fusion | flops 1851360 | bytes 2468480 | tf_op jit(solution)/shard_map/concatenate | solution.py:19
  38.2 3.7 %fusion.3 = f32[25,74,138]{2,1,0:T(8,128)S(1)} fusion(f32[29,76,140]{2,1,0:T(8,128)S(1)} %pad_maximum_fusion, f32[25]{0:T(128)S(1)} %get-tuple-element.31, f32[74,138]{1,0:T(8,128)S(1)} %get-tuple-element.9, f32[25]{0:T(128)S(1)} %get-tuple-element.32, f32[74,138]{1,0:T(8,128)S(1)} %maximum_bitcast_fusion.1, f32[25]{0:T(128)S(1)} %get-tuple-element.30, ...), kind=kLoop, calls=%fused_computation.8 | loop fusion | flops 5106000 | bytes 10375792 | tf_op jit(solution)/shard_map/mul | solution.py:31
  42.9 3.3 %fusion.17 = f32[25,72,136]{2,1,0:T(8,128)S(1)} fusion(f32[25,74,138]{2,1,0:T(8,128)S(1)} %fusion.3, f32[25]{0:T(128)S(1)} %get-tuple-element.31, f32[72,136]{1,0:T(8,128)S(1)} %get-tuple-element.7, f32[25]{0:T(128)S(1)} %get-tuple-element.32, f32[72,136]{1,0:T(8,128)S(1)} %maximum_bitcast_fusion.7, f32[25]{0:T(128)S(1)} %get-tuple-element.30, ...), kind=kLoop, calls=%fused_computation.36 | loop fusion | flops 4896000 | bytes 9949072 | tf_op jit(solution)/shard_map/mul | solution.py:31
  47.2 3.3 %fusion.10 = f32[25,70,134]{2,1,0:T(8,128)S(1)} fusion(f32[25,72,136]{2,1,0:T(8,128)S(1)} %fusion.17, f32[25]{0:T(128)S(1)} %get-tuple-element.31, f32[70,134]{1,0:T(8,128)S(1)} %get-tuple-element.5, f32[25]{0:T(128)S(1)} %get-tuple-element.32, f32[70,134]{1,0:T(8,128)S(1)} %maximum_bitcast_fusion.4, f32[25]{0:T(128)S(1)} %get-tuple-element.30, ...), kind=kLoop, calls=%fused_computation.22 | loop fusion | flops 4690000 | bytes 9530480 | tf_op jit(solution)/shard_map/mul | solution.py:31
  53.2 2.1 %stack.16 = f32[1,25,2948]{2,1,0:T(8,128)} reshape(f32[25,22,134]{2,1,0:T(8,128)} %get-tuple-element.15) | data formatting | bytes 589600 | tf_op jit(solution)/shard_map/stack | solution.py:79
  55.3 2.1 %stack.17 = f32[1,25,2948]{2,1,0:T(8,128)} reshape(f32[25,22,134]{2,1,0:T(8,128)} %get-tuple-element.14) | data formatting | bytes 589600 | tf_op jit(solution)/shard_map/stack | solution.py:79
  58.3 2.6 %pad_maximum_fusion.1 = f32[4,25,2948]{2,1,0:T(8,128)} fusion(f32[1,25,2948]{2,1,0:T(8,128)} %stack.18, f32[1,25,2948]{2,1,0:T(8,128)} %stack.17, f32[1,25,2948]{2,1,0:T(8,128)} %stack.16, f32[1,25,2948]{2,1,0:T(8,128)S(1)} %stack.15), kind=kLoop, calls=%fused_computation.47 | loop fusion | flops 884400 | bytes 2358400 | tf_op jit(solution)/shard_map/stack | solution.py:79
  60.9 8.0 %all-to-all-start = ((f32[4,25,2948]{2,1,0:T(8,128)}), f32[4,25,2948]{2,1,0:T(8,128)}, u32[]{:S(2)}, u32[]{:S(2)}) async-start(f32[4,25,2948]{2,1,0:T(8,128)} %pad_maximum_fusion.1), calls=%async_computation | async-start | bytes 3145728 | tf_op jit(solution)/shard_map/all_to_all | solution.py:83
  68.9 1.7 %convolution_bitcast_fusion.2 = f32[8,8,2048,1]{2,1,3,0:T(8,128)} fusion(s32[2048]{0:T(1024)S(1)} %iota_add_fusion, s32[256]{0:T(256)S(1)} %copy-done.13, f32[256]{0:T(256)S(1)} %copy-done.14, s32[256]{0:T(256)S(1)} %copy-done.15), kind=kOutput, calls=%fused_computation.3 | convolution fusion | flops 403210240 | bytes 535552 | tf_op jit(solution)/shard_map/dot_general | solution.py:65
  72.0 16.2 %all-to-all-done = f32[4,25,2948]{2,1,0:T(8,128)} async-done(((f32[4,25,2948]{2,1,0:T(8,128)}), f32[4,25,2948]{2,1,0:T(8,128)}, u32[]{:S(2)}, u32[]{:S(2)}) %all-to-all-start) | async-done | bytes 1179232 | tf_op jit(solution)/shard_map/all_to_all | solution.py:83
  92.3 1.9 %fusion.25 = f32[100,20,132]{0,2,1:T(8,128)S(1)} fusion(f32[100,22,134]{0,2,1:T(8,128)S(1)} %fusion.22, f32[100]{0:T(128)S(1)} %get-tuple-element.28, f32[20,132]{1,0:T(8,128)S(1)} %get-tuple-element.25, f32[100]{0:T(128)S(1)} %get-tuple-element.29, f32[20,132]{1,0:T(8,128)S(1)} %get-tuple-element.26, f32[100]{0:T(128)S(1)} %get-tuple-element.27, ...), kind=kLoop, calls=%fused_computation.53 | loop fusion | flops 5280000 | bytes 10603440 | tf_op jit(solution)/shard_map/mul | solution.py:31
  94.2 1.8 %fusion.32 = f32[100,18,130]{0,2,1:T(8,128)S(1)} fusion(f32[100,20,132]{0,2,1:T(8,128)S(1)} %fusion.25, f32[100]{0:T(128)S(1)} %get-tuple-element.28, f32[18,130]{1,0:T(8,128)S(1)} %get-tuple-element.22, f32[100]{0:T(128)S(1)} %get-tuple-element.29, f32[18,130]{1,0:T(8,128)S(1)} %get-tuple-element.23, f32[100]{0:T(128)S(1)} %get-tuple-element.27, ...), kind=kLoop, calls=%fused_computation.68 | loop fusion | flops 4680000 | bytes 9398640 | tf_op jit(solution)/shard_map/mul | solution.py:31
  100.0 2.3 %slice_add_fusion.15 = (f32[100,16,128]{0,2,1:T(8,128)}, f32[100,16,128]{0,2,1:T(8,128)S(1)}) fusion(f32[100,22,134]{0,2,1:T(8,128)S(1)} %fusion.22, f32[100,16,128]{0,2,1:T(8,128)} %bitcast.81, s32[16,128]{1,0:T(8,128)S(1)} %slice.443), kind=kLoop, calls=%fused_computation.81 | loop fusion | flops 614400 | bytes 3284992 | tf_op jit(solution)/shard_map/add | solution.py:92
  102.2 1.7 %copy.71 = f32[100,16,128]{2,1,0:T(8,128)S(1)} copy(f32[100,16,128]{0,2,1:T(8,128)} %get-tuple-element.2) | data formatting | bytes 1638400 | tf_op jit(solution)/shard_map/add | solution.py:92
  104.1 3.7 %convolution_bitcast_fusion.3 = f32[8,4,8,25]{3,2,1,0:T(8,128)S(1)} fusion(f32[8,8,2048,1]{2,1,3,0:T(8,128)} %convolution_bitcast_fusion.2, f32[4,25,2048,1]{2,1,0,3:T(8,128)S(1)} %reshape.67), kind=kOutput, calls=%fused_computation.80 | convolution fusion | flops 157286400 | bytes 1369088 | tf_op jit(solution)/shard_map/dot_general | solution.py:95
  108.6 3.6 %all-to-all-start.2 = ((f32[32,1,200]{2,1,0:T(1,128)}), f32[32,1,200]{2,1,0:T(1,128)S(1)}, u32[]{:S(2)}, u32[]{:S(2)}) async-start(f32[32,1,200]{2,1,0:T(1,128)} %all_to_all.29), calls=%async_computation.2 | async-start | bytes 65536 | tf_op jit(solution)/shard_map/all_to_all | solution.py:100
  113.4 5.8 %all-to-all-done.2 = f32[32,1,200]{2,1,0:T(1,128)S(1)} async-done(((f32[32,1,200]{2,1,0:T(1,128)}), f32[32,1,200]{2,1,0:T(1,128)S(1)}, u32[]{:S(2)}, u32[]{:S(2)}) %all-to-all-start.2) | async-done | bytes 25632 | tf_op jit(solution)/shard_map/all_to_all | solution.py:100
  119.2 3.9 %all-to-all-start.1 = ((f32[100,16,128]{2,1,0:T(8,128)}), f32[100,16,128]{2,1,0:T(8,128)S(1)}, u32[]{:S(2)}, u32[]{:S(2)}) async-start(f32[100,16,128]{2,1,0:T(8,128)} %copy.69), calls=%async_computation.1 | async-start | bytes 1638400 | tf_op jit(solution)/shard_map/all_to_all | solution.py:93
  123.8 10.4 %all-to-all-done.1 = f32[100,16,128]{2,1,0:T(8,128)S(1)} async-done(((f32[100,16,128]{2,1,0:T(8,128)}), f32[100,16,128]{2,1,0:T(8,128)S(1)}, u32[]{:S(2)}, u32[]{:S(2)}) %all-to-all-start.1) | async-done | bytes 819232 | tf_op jit(solution)/shard_map/all_to_all | solution.py:93
  (89 shorter events, 37.1 us)
Async XLA Ops:
  0.6 89.1 %copy-start = (f32[100,100]{1,0:T(8,128)S(1)}, f32[100,100]{1,0:T(8,128)}, u32[]{:S(2)}) copy-start(f32[100,100]{1,0:T(8,128)} %param.12) | copy-start | bytes 120004
  4.0 6.1 %copy-start.12 = (f32[3,100]{1,0:T(4,128)S(1)}, f32[3,100]{1,0:T(4,128)}, u32[]{:S(2)}) copy-start(f32[3,100]{1,0:T(4,128)} %param.10) | copy-start | bytes 3604
  4.0 10.5 %copy-start.7 = (f32[3,64,128]{2,1,0:T(8,128)S(1)}, f32[3,64,128]{2,1,0:T(8,128)}, u32[]{:S(2)}) copy-start(f32[3,64,128]{2,1,0:T(8,128)} %param.9) | copy-start | bytes 294916
  4.4 5.8 %collective-permute-start = (f32[29,64,6]{1,0,2:T(8,128)S(1)}, f32[29,64,6]{1,0,2:T(8,128)S(1)}, u32[]{:S(2)}, u32[]{:S(2)}) collective-permute-start(f32[29,64,6]{1,0,2:T(8,128)S(1)} %copy.47), channel_id=1, source_target_pairs={{0,16},{1,17},{2,18},{3,19},{4,20},{5,21},{6,22},{7,23},{8,24},{9,... | collective-permute-start | bytes 133640 | tf_op jit(solution)/shard_map/ppermute | solution.py:15
  8.8 5.4 %collective-permute-start.1 = (f32[29,64,6]{1,0,2:T(8,128)S(1)}, f32[29,64,6]{1,0,2:T(8,128)S(1)}, u32[]{:S(2)}, u32[]{:S(2)}) collective-permute-start(f32[29,64,6]{1,0,2:T(8,128)S(1)} %copy.48), channel_id=1, source_target_pairs={{16,0},{17,1},{18,2},{19,3},{20,4},{21,5},{22,6},{23,7},{24,8},{25... | collective-permute-start | bytes 133640 | tf_op jit(solution)/shard_map/ppermute | solution.py:18
  10.6 24.1 %copy-start.1 = (f32[29,64,6]{2,1,0:T(8,128)}, f32[29,64,6]{2,1,0:T(8,128)S(1)}, u32[]{:S(2)}) copy-start(f32[29,64,6]{2,1,0:T(8,128)S(1)} %copy.49) | copy-start | bytes 133636
  14.5 20.2 %copy-start.3 = (f32[29,64,6]{2,1,0:T(8,128)}, f32[29,64,6]{2,1,0:T(8,128)S(1)}, u32[]{:S(2)}) copy-start(f32[29,64,6]{2,1,0:T(8,128)S(1)} %copy.50) | copy-start | bytes 133636
  15.6 6.5 %collective-permute-start.2 = (f32[29,6,140]{2,1,0:T(8,128)}, f32[29,6,140]{2,1,0:T(8,128)S(1)}, u32[]{:S(2)}, u32[]{:S(2)}) collective-permute-start(f32[29,6,140]{2,1,0:T(8,128)} %get-tuple-element.10), channel_id=1, source_target_pairs={{0,4},{4,8},{8,12},{1,5},{5,9},{9,13},{2,6},{6,10},{10,14},{3,7},{... | collective-permute-start | bytes 292328 | tf_op jit(solution)/shard_map/ppermute | solution.py:15
  18.8 7.1 %collective-permute-start.3 = (f32[29,6,140]{2,1,0:T(8,128)}, f32[29,6,140]{2,1,0:T(8,128)S(1)}, u32[]{:S(2)}, u32[]{:S(2)}) collective-permute-start(f32[29,6,140]{2,1,0:T(8,128)} %get-tuple-element.11), channel_id=1, source_target_pairs={{4,0},{8,4},{12,8},{5,1},{9,5},{13,9},{6,2},{10,6},{14,10},{7,3},{... | collective-permute-start | bytes 292328 | tf_op jit(solution)/shard_map/ppermute | solution.py:18
  25.9 8.8 %copy-start.5 = (f32[29,6,140]{2,1,0:T(8,128)}, f32[29,6,140]{2,1,0:T(8,128)S(1)}, u32[]{:S(2)}) copy-start(f32[29,6,140]{2,1,0:T(8,128)S(1)} %collective-permute-done.3) | copy-start | bytes 292324
  34.7 0.9 copy-start.8
  35.6 2.6 %copy-start.9 = (s32[74,138]{1,0:T(8,128)S(1)}, s32[74,138]{1,0:T(8,128)}, u32[]{:S(2)}) copy-start(s32[74,138]{1,0:T(8,128)} %copy.54) | copy-start | bytes 122548
  38.2 3.7 %copy-start.2 = (f32[29,64,6]{2,1,0:T(8,128)S(1)}, f32[29,64,6]{2,1,0:T(8,128)}, u32[]{:S(2)}) copy-start(f32[29,64,6]{2,1,0:T(8,128)} %copy-done.1) | copy-start | bytes 133636
  38.2 3.7 %copy-start.4 = (f32[29,64,6]{2,1,0:T(8,128)S(1)}, f32[29,64,6]{2,1,0:T(8,128)}, u32[]{:S(2)}) copy-start(f32[29,64,6]{2,1,0:T(8,128)} %copy-done.3) | copy-start | bytes 133636
  38.2 3.7 %copy-start.6 = (f32[29,6,140]{2,1,0:T(8,128)S(1)}, f32[29,6,140]{2,1,0:T(8,128)}, u32[]{:S(2)}) copy-start(f32[29,6,140]{2,1,0:T(8,128)} %copy-done.5) | copy-start | bytes 292324
  42.0 0.9 copy-start.11
  46.3 0.9 copy-start.10
  60.9 8.0 %copy-start.13 = (s32[256]{0:T(256)S(1)}, s32[256]{0:T(256)}, u32[]{:S(2)}) copy-start(s32[256]{0:T(256)} %param.13) | copy-start | bytes 3076
  60.9 8.0 %copy-start.14 = (f32[256]{0:T(256)S(1)}, f32[256]{0:T(256)}, u32[]{:S(2)}) copy-start(f32[256]{0:T(256)} %param.15) | copy-start | bytes 3076
  60.9 8.0 %copy-start.15 = (s32[256]{0:T(256)S(1)}, s32[256]{0:T(256)}, u32[]{:S(2)}) copy-start(s32[256]{0:T(256)} %param.14) | copy-start | bytes 3076
  60.9 27.3 %all-to-all-start = ((f32[4,25,2948]{2,1,0:T(8,128)}), f32[4,25,2948]{2,1,0:T(8,128)}, u32[]{:S(2)}, u32[]{:S(2)}) async-start(f32[4,25,2948]{2,1,0:T(8,128)} %pad_maximum_fusion.1), calls=%async_computation | async-start | bytes 3145728 | tf_op jit(solution)/shard_map/all_to_all | solution.py:83
  108.6 10.7 %all-to-all-start.2 = ((f32[32,1,200]{2,1,0:T(1,128)}), f32[32,1,200]{2,1,0:T(1,128)S(1)}, u32[]{:S(2)}, u32[]{:S(2)}) async-start(f32[32,1,200]{2,1,0:T(1,128)} %all_to_all.29), calls=%async_computation.2 | async-start | bytes 65536 | tf_op jit(solution)/shard_map/all_to_all | solution.py:100
  119.2 15.0 %all-to-all-start.1 = ((f32[100,16,128]{2,1,0:T(8,128)}), f32[100,16,128]{2,1,0:T(8,128)S(1)}, u32[]{:S(2)}, u32[]{:S(2)}) async-start(f32[100,16,128]{2,1,0:T(8,128)} %copy.69), calls=%async_computation.1 | async-start | bytes 1638400 | tf_op jit(solution)/shard_map/all_to_all | solution.py:93

commit v2 on v1

v2 whole, which is shorter than its diff:
```python
import jax
import jax.numpy as jnp
from jax import lax
from jax.experimental import pallas as pl
from jax.experimental.pallas import tpu as pltpu
from jax.sharding import PartitionSpec as P

NSUB = 3
G_DEV = 8
HI = lax.Precision.HIGHEST


def extended(block, axis, dim, width):
    count = lax.axis_size(axis)
    forward = [(i, i + 1) for i in range(count - 1)]
    backward = [(target, source) for source, target in forward]
    low = lax.ppermute(
        lax.slice_in_dim(block, block.shape[dim] - width, None, axis=dim), axis, forward
    )
    high = lax.ppermute(lax.slice_in_dim(block, 0, width, axis=dim), axis, backward)
    return jnp.concatenate([low, block, high], axis=dim)

LANES = 128
VMEM = pl.BlockSpec(memory_space=pltpu.VMEM)
SMEM = pl.BlockSpec(memory_space=pltpu.SMEM)
OFF = 4
PARAMS = pltpu.CompilerParams(vmem_limit_bytes=48 * 1024 * 1024)


def substeps(a, wet, kx, ky, ks):
    kx, ky, ks = wet * kx, wet * ky, wet * (0.25 * ks)
    rows, lanes = a.shape
    for _ in range(NSUB):
        east, west = pltpu.roll(a, lanes - 1, 1), pltpu.roll(a, 1, 1)
        north, south = pltpu.roll(a, rows - 1, 0), pltpu.roll(a, 1, 0)
        slope = east - west
        cross = pltpu.roll(slope, rows - 1, 0) - pltpu.roll(slope, 1, 0)
        twice = 2.0 * a
        a = wet * a + kx * (east - twice + west) + ky * (north - twice + south) + ks * cross
    return a


def levels_kernel(local, parts, col_rows, base_ref, cv_ref, p_ref, out_ref, side):
    tiles = (col_rows + 8) // 8
    coefs = [p_ref.at[local + c] for c in range(3)]

    def level(l, carry):
        k = (base_ref[0] + l).astype(jnp.float32)
        wet = jnp.where(k < p_ref[local + 3], 1.0, 0.0)
        a = substeps(p_ref[l], wet, *(c[...] * cv_ref[i, l] for i, c in enumerate(coefs)))
        for part in range(parts):
            for t in range(tiles):
                row = part * col_rows + 8 * t
                out_ref[part, tiles * l + t] = a[row : row + 8, :LANES]
        side[l] = a[:, LANES:]
        return carry

    lax.fori_loop(0, local, level, 0)
    lane = lax.broadcasted_iota(jnp.int32, (8, LANES), 1)

    def pack(q, carry):
        for part in range(parts):
            acc = jnp.zeros((8, LANES), jnp.float32)
            for j in range(5):
                for t in range(tiles):
                    slot = 8 * (tiles * j + t)
                    row = part * col_rows + 8 * t
                    tile = pltpu.roll(side[5 * q + j, row : row + 8, :], slot + NSUB, 1)
                    acc = jnp.where((lane >= slot) & (lane < slot + 2 * NSUB), tile, acc)
            out_ref[part, tiles * local + q] = acc
        return carry

    lax.fori_loop(0, local // 5, pack, 0)


def split(x):
    high = x.astype(jnp.bfloat16)
    return high, (x - high.astype(jnp.float32)).astype(jnp.bfloat16)


def columns_kernel(local, parts, col_rows, cv_ref, inv_ref, c_ref, m_ref, in_ref,
                   out_ref, flux_ref, main, side, after):
    levels = local * parts
    tall = col_rows + 8
    tiles = tall // 8
    lane = lax.broadcasted_iota(jnp.int32, (8, LANES), 1)
    rim = (lane < NSUB) | (lane >= LANES - NSUB)

    def unpack(q, carry):
        for part in range(parts):
            packed = in_ref[part, tiles * local + q]
            for j in range(5):
                for t in range(tiles):
                    shift = LANES - NSUB - 8 * (tiles * j + t)
                    row = pl.multiple_of((part * local + 5 * q + j) * tall + 8 * t, 8)
                    side[pl.ds(row, 8), :] = jnp.where(rim, pltpu.roll(packed, shift, 1), 0.0)
                    main[pl.ds(row, 8), :] = in_ref[part, tiles * (5 * q + j) + t]
        return carry

    lax.fori_loop(0, local // 5, unpack, 0)
    inv_high, inv_low = split(inv_ref[...])
    ids = lax.broadcasted_iota(jnp.int32, (levels, 2 * LANES), 0).astype(jnp.float32)

    def solve(field, bounds):
        high, low = split(field)
        dot = lambda a, b: jnp.dot(a, b, preferred_element_type=jnp.float32)
        out = dot(inv_high, high) + (dot(inv_low, high) + dot(inv_high, low))
        return jnp.where(ids < bounds, out, 0.0)

    for r in range(1, tall - 1):
        at = pl.ds(r, levels, stride=tall)
        field = jnp.concatenate([main[at, :], side[at, :]], axis=1)
        field = solve(field, c_ref[3, r : r + 1, :])
        main[at, :] = field[:, :LANES]
        side[at, :] = field[:, LANES:]

    def level(k, carry):
        at = pl.ds(pl.multiple_of(k * tall, 8), tall)
        wet = jnp.where(k.astype(jnp.float32) < c_ref[3], 1.0, 0.0)
        a = jnp.concatenate([main[at, :], side[at, :]], axis=1)
        a = substeps(a, wet, *(c_ref[i] * cv_ref[i, k] for i in range(3)))
        after[at, :] = a[:, :LANES]
        return carry

    lax.fori_loop(0, levels, level, 0)
    flux = jnp.zeros(flux_ref.shape, jnp.float32)
    for r in range(0, col_rows, 2):
        ats = [pl.ds(OFF + r + i, levels, stride=tall) for i in range(2)]
        bounds = [c_ref[3, OFF + r + i : OFF + r + i + 1, :LANES] for i in range(2)]
        field = jnp.concatenate([after[at, :] for at in ats], axis=1)
        field = solve(field, jnp.concatenate(bounds, axis=1))
        for i in range(2):
            half = field[:, i * LANES : (i + 1) * LANES]
            out_ref[pl.ds(r + i, levels, stride=col_rows), :] = half
            cells = m_ref[:, (r + i) * LANES : (r + i + 1) * LANES]
            flux += lax.dot_general(
                cells, half + main[ats[i], :], (((1,), (1,)), ((), ())), precision=HI,
                preferred_element_type=jnp.float32,
            )
    flux_ref[...] = flux


def per_device(tracer_in, coef_h, coef_v, wet_levels, column_inv, sec_cell, sec_gate, sec_weight):
    depth_count = lax.axis_size("gz")
    depth_index = lax.axis_index("gz")
    tiles = lax.axis_size(("tx", "ty"))
    local_levels, rows, width = tracer_in.shape
    levels = local_levels * depth_count
    col_rows = rows // depth_count
    tall = col_rows + 8
    level_ids = depth_index * local_levels + jnp.arange(local_levels, dtype=jnp.int32)
    coef_depth = lax.dynamic_slice_in_dim(coef_v, depth_index * local_levels, local_levels, 1)
    row_start = depth_index * col_rows

    gate_ids = jnp.arange(G_DEV * tiles, dtype=jnp.int32)
    gate_hot = jnp.where(gate_ids[:, None] == sec_gate[None, :], sec_weight[None, :], 0.0)
    cells = row_start * width + jnp.arange(col_rows * width, dtype=jnp.int32)
    cell_hot = (sec_cell[:, None] == cells[None, :]).astype(jnp.float32)
    gate_cells = jnp.dot(gate_hot, cell_hot, precision=HI)

    rim = 2 * NSUB
    wet_depth = (level_ids[:, None, None] < wet_levels[None]).astype(jnp.float32)
    packed = jnp.concatenate(
        [wet_depth * tracer_in, coef_h, wet_levels[None].astype(jnp.float32)], axis=0
    )
    packed = extended(extended(packed, "tx", 2, rim), "ty", 1, rim)
    channels = packed.shape[0]
    gap = jnp.zeros((channels, packed.shape[1], 2 * LANES - packed.shape[2]), jnp.float32)
    packed = jnp.concatenate([packed[:, :, rim:], gap, packed[:, :, :rim]], axis=2)
    gap = jnp.zeros((channels, 2 * OFF + rows + 8 - packed.shape[1], 2 * LANES), jnp.float32)
    packed = jnp.concatenate([packed[:, rim - OFF :], gap, packed[:, : rim - OFF]], axis=1)

    count = local_levels * tall // 8 + local_levels // 5
    sent = pl.pallas_call(
        lambda *refs: levels_kernel(local_levels, depth_count, col_rows, *refs),
        out_shape=jax.ShapeDtypeStruct((depth_count, count, 8, LANES), jnp.float32),
        in_specs=[SMEM, SMEM, VMEM],
        out_specs=VMEM,
        scratch_shapes=[pltpu.VMEM((local_levels, packed.shape[1], LANES), jnp.float32)],
        compiler_params=PARAMS,
    )((depth_index * local_levels)[None].astype(jnp.int32), coef_depth, packed)
    got = lax.all_to_all(sent, "gz", split_axis=0, concat_axis=0, tiled=True)

    window = lax.dynamic_slice_in_dim(packed[local_levels:], row_start, tall, 1)
    field, flux = pl.pallas_call(
        lambda *refs: columns_kernel(local_levels, depth_count, col_rows, *refs),
        out_shape=(
            jax.ShapeDtypeStruct((levels * col_rows, LANES), jnp.float32),
            jax.ShapeDtypeStruct((G_DEV * tiles, levels), jnp.float32),
        ),
        in_specs=[SMEM, VMEM, VMEM, VMEM, VMEM],
        out_specs=(VMEM, VMEM),
        scratch_shapes=[pltpu.VMEM((levels * tall, LANES), jnp.float32)] * 3,
        compiler_params=PARAMS,
    )(coef_v, column_inv.T, window, gate_cells, got)
    field = field.reshape(levels, col_rows, width)
    out = lax.all_to_all(field, "gz", split_axis=0, concat_axis=1, tiled=True)
    flux = flux.reshape(tiles, G_DEV, depth_count, local_levels).transpose(0, 2, 1, 3)
    flux = flux.reshape(tiles * depth_count, G_DEV * local_levels)
    flux = lax.all_to_all(flux, ("tx", "ty", "gz"), split_axis=0, concat_axis=0, tiled=True)
    flux = jnp.sum(flux, axis=0).reshape(G_DEV, local_levels)
    return (out, flux)


def solution(mesh):
    in_specs = (
        P("gz", "ty", "tx"),
        P(None, "ty", "tx"),
        P(),
        P("ty", "tx"),
        P(),
        P(("tx", "ty")),
        P(("tx", "ty")),
        P(("tx", "ty")),
    )
    out_specs = (P("gz", "ty", "tx"), P(("tx", "ty"), "gz"))
    return jax.shard_map(
        per_device, mesh=mesh, in_specs=in_specs, out_specs=out_specs, check_vma=False
    )
```

time: 137 us -> 126 us (0.920)
  Pallas kernels: 0 us -> 45.2 us
  other arithmetic: 29.2 us -> 4.99 us
  local copies, waits for them, and re-layouts: 30.3 us -> 6.24 us
  blocking collectives: 0 us -> 10.5 us
  matrix products: 7.82 us -> 0.91 us
  waiting for transfers between devices: 41.7 us -> 34.8 us
  starting transfers between devices: 25.1 us -> 21.4 us
    pallas_call x0 -> x2, Pallas kernels: none -> 45.2 us  [the longest x1 33.9 us: per_device(): pl.pallas_call(lambda *refs: columns_kernel(local_levels, depth_count, co...]
    mul x13 -> x0, other arithmetic: 16.9 us -> none  [the longest x6 15.5 us: diffuse(): wet * (centre + coef_x * along_x + coef_y * along_y + 0.25 * coef_s * cross)]
    all_to_all x0 -> x1, blocking collectives: none -> 10.5 us  [per_device(): lax.all_to_all(flux, ('tx', 'ty', 'gz'), split_axis=0, concat_axis=0, til...]
    another operation x5 -> x0, local copies, waits for them, and re-layouts: 8.01 us -> none  [the longest x4 6.45 us: per_device(): jnp.stack([field[:, part * col_rows:part * col_rows + tall, :] for part i...]
    slice x12 -> x5, local copies, waits for them, and re-layouts: 8.6 us -> 1.01 us  [the longest x1 0.68 us: per_device(): packed[:, :, rim:]]
    all_to_all x2 -> x1, waiting for transfers between devices: 22 us -> 15.4 us  [per_device(): got = lax.all_to_all(sent, 'gz', split_axis=0, concat_axis=0, tiled=True)]
    dot_general x3 -> x0, matrix products: 6.12 us -> none  [the longest x1 3.74 us: per_device(): lax.dot_general(gate_cells, total.reshape(levels, -1), (((1,), (1,)), (()...]
    all_to_all x2 -> x1, starting transfers between devices: 11.5 us -> 7.78 us  [per_device(): got = lax.all_to_all(sent, 'gz', split_axis=0, concat_axis=0, tiled=True)]
  transfers between devices with their start and end apart: 7 -> 6, of which waited for: 6 -> 5; matrix products, arithmetic and copies ran while one was open for 4% -> 2% of each run, Pallas kernels for 0% -> 0%
where the time goes in v2:
time: 126 us; the launch traced here: 125 us
  Pallas kernels  45.2 us (36%)
  waiting for transfers between devices  34.8 us (28%)
  starting transfers between devices  21.4 us (17%)
  blocking collectives  10.5 us (8%)
  local copies, waits for them, and re-layouts  6.24 us (5%)
  other arithmetic  4.99 us (4%)
    pallas_call x1, Pallas kernels, per_device(): pl.pallas_call(lambda *refs: columns_kernel(local_levels, depth_count, co...  33.9 us
    all_to_all x1, waiting for transfers between devices, per_device(): got = lax.all_to_all(sent, 'gz', split_axis=0, concat_axis=0, tiled=True)  15.4 us
    pallas_call x1, Pallas kernels, per_device(): pl.pallas_call(lambda *refs: levels_kernel(local_levels, depth_count, col...  11.2 us
    all_to_all x1, blocking collectives, per_device(): lax.all_to_all(flux, ('tx', 'ty', 'gz'), split_axis=0, concat_axis=0, til...  10.5 us
    all_to_all x1, waiting for transfers between devices, per_device(): out = lax.all_to_all(field, 'gz', split_axis=0, concat_axis=1, tiled=True)  10.4 us
    all_to_all x1, starting transfers between devices, per_device(): got = lax.all_to_all(sent, 'gz', split_axis=0, concat_axis=0, tiled=True)  7.78 us
    ppermute x2, waiting for transfers between devices, extended(): lax.ppermute(lax.slice_in_dim(block, 0, width, axis=dim), axis, backward)  7.33 us
    ppermute x2, starting transfers between devices, extended(): lax.ppermute(lax.slice_in_dim(block, block.shape[dim] - width, None, axis...  7.19 us
  transfers between devices with their start and end apart: 6, of which 5 were waited for; matrix products, arithmetic and copies ran while one was open for 2% of the time, Pallas kernels for 0%

profile of v2, /device:TPU:1, one launch (start us, length us, event | category | flops | bytes accessed | tf_op | source)
XLA Modules:
  0.0 124.9 jit_solution(17929094678472398871)
XLA Ops:
  0.6 0.8 convert_bitcast_fusion
  1.4 1.3 %compare_select_fusion = f32[25,64,128]{2,1,0:T(8,128)S(1)} fusion(f32[25,64,128]{2,1,0:T(8,128)} %param.8, s32[64,128]{1,0:T(8,128)} %param.11, s32[25]{0:T(128)S(1)} %iota_add_fusion.1), kind=kLoop, calls=%fused_computation.8 | loop fusion | flops 409600 | bytes 1671268 | tf_op jit(solution)/shard_map/mul | solution.py:164
  2.7 1.0 pad_maximum_fusion.3
  4.4 4.0 %collective-permute-start = (f32[29,64,6]{1,0,2:T(8,128)S(1)}, f32[29,64,6]{1,0,2:T(8,128)S(1)}, u32[]{:S(2)}, u32[]{:S(2)}) collective-permute-start(f32[29,64,6]{1,0,2:T(8,128)S(1)} %copy.16), channel_id=1, source_target_pairs={{0,16},{1,17},{2,18},{3,19},{4,20},{5,21},{6,22},{7,23},{8,24},{9,... | collective-permute-start | bytes 133640 | tf_op jit(solution)/shard_map/ppermute | solution.py:17
  8.8 1.3 %collective-permute-start.1 = (f32[29,64,6]{1,0,2:T(8,128)S(1)}, f32[29,64,6]{1,0,2:T(8,128)S(1)}, u32[]{:S(2)}, u32[]{:S(2)}) collective-permute-start(f32[29,64,6]{1,0,2:T(8,128)S(1)} %copy.17), channel_id=1, source_target_pairs={{16,0},{17,1},{18,2},{19,3},{20,4},{21,5},{22,6},{23,7},{24,8},{25... | collective-permute-start | bytes 133640 | tf_op jit(solution)/shard_map/ppermute | solution.py:20
  10.6 3.5 %collective-permute-done.1 = f32[29,64,6]{1,0,2:T(8,128)S(1)} collective-permute-done((f32[29,64,6]{1,0,2:T(8,128)S(1)}, f32[29,64,6]{1,0,2:T(8,128)S(1)}, u32[]{:S(2)}, u32[]{:S(2)}) %collective-permute-start.1) | collective-permute-done | bytes 44576 | tf_op jit(solution)/shard_map/ppermute | solution.py:20
  14.8 3.2 %collective-permute-start.2 = (f32[29,6,140]{2,1,0:T(8,128)S(1)}, f32[29,6,140]{2,1,0:T(8,128)S(1)}, u32[]{:S(2)}, u32[]{:S(2)}) collective-permute-start(f32[29,6,140]{2,1,0:T(8,128)S(1)} %get-tuple-element.6), channel_id=1, source_target_pairs={{0,4},{4,8},{8,12},{1,5},{5,9},{9,13},{2,6},{6,10},{10,14},{3,7},{... | collective-permute-start | bytes 292328 | tf_op jit(solution)/shard_map/ppermute | solution.py:17
  18.0 1.3 %collective-permute-start.3 = (f32[29,6,140]{2,1,0:T(8,128)S(1)}, f32[29,6,140]{2,1,0:T(8,128)S(1)}, u32[]{:S(2)}, u32[]{:S(2)}) collective-permute-start(f32[29,6,140]{2,1,0:T(8,128)S(1)} %get-tuple-element.7), channel_id=1, source_target_pairs={{4,0},{8,4},{12,8},{5,1},{9,5},{13,9},{6,2},{10,6},{14,10},{7,3},{... | collective-permute-start | bytes 292328 | tf_op jit(solution)/shard_map/ppermute | solution.py:20
  19.4 1.6 %collective-permute-done.2 = f32[29,6,140]{2,1,0:T(8,128)S(1)} collective-permute-done((f32[29,6,140]{2,1,0:T(8,128)S(1)}, f32[29,6,140]{2,1,0:T(8,128)S(1)}, u32[]{:S(2)}, u32[]{:S(2)}) %collective-permute-start.2) | collective-permute-done | bytes 97472 | tf_op jit(solution)/shard_map/ppermute | solution.py:17
  21.0 3.8 %collective-permute-done.3 = f32[29,6,140]{2,1,0:T(8,128)S(1)} collective-permute-done((f32[29,6,140]{2,1,0:T(8,128)S(1)}, f32[29,6,140]{2,1,0:T(8,128)S(1)}, u32[]{:S(2)}, u32[]{:S(2)}) %collective-permute-start.3) | collective-permute-done | bytes 97472 | tf_op jit(solution)/shard_map/ppermute | solution.py:20
  24.8 0.9 pad_maximum_fusion
  25.7 0.7 slice.38
  26.5 0.4 pad_maximum_fusion.1
  27.6 11.2 %shard_map.95 = f32[4,80,8,128]{3,2,1,0:T(8,128)S(1)} custom-call(s32[1]{0:T(128)} %bitcast.2.refs_0_, f32[3,25]{1,0:T(4,128)S(1)} %constant_dynamic-slice_fusion.refs_1_, f32[29,80,256]{2,1,0:T(8,128)S(1)} %pad_maximum_fusion.2.refs_2_), custom_call_target="tpu_custom_call" | custom-call | tf_op jit(solution)/shard_map/pallas_call | solution.py:174
  38.9 1.1 copy-done
  39.9 7.8 %all-to-all-start = ((f32[4,80,8,128]{3,2,1,0:T(8,128)}), f32[4,80,8,128]{3,2,1,0:T(8,128)}, u32[]{:S(2)}, u32[]{:S(2)}) async-start(f32[4,80,8,128]{3,2,1,0:T(8,128)} %copy-done), calls=%async_computation | async-start | bytes 2621440 | tf_op jit(solution)/shard_map/all_to_all | solution.py:182
  47.8 0.9 fusion.refs_3_
  48.8 15.4 %all-to-all-done.refs_4_ = f32[4,80,8,128]{3,2,1,0:T(8,128)} async-done(((f32[4,80,8,128]{3,2,1,0:T(8,128)}), f32[4,80,8,128]{3,2,1,0:T(8,128)}, u32[]{:S(2)}, u32[]{:S(2)}) %all-to-all-start) | async-done | bytes 1310752 | tf_op jit(solution)/shard_map/all_to_all | solution.py:182
  64.2 33.9 %shard_map.96 = (f32[1600,128]{1,0:T(8,128)}, f32[64,100]{1,0:T(8,128)S(1)}) custom-call(f32[3,100]{1,0:T(4,128)S(1)} %copy-done.1, f32[100,100]{1,0:T(8,128)S(1)} %bitcast.14, f32[4,24,256]{2,1,0:T(8,128)S(1)} %constant_dynamic-slice_fusion.1.refs_2_, f32[64,2048]{1,0:T(8,128)S(1)} %fusion.refs_3_, f32[4,80,8,128]{3,2,1,0:T(8,128)} %all-to-all-done.refs_4_), custom_call_target="tpu_custom_call" | custom-call | tf_op jit(solution)/shard_map/pallas_call | solution.py:185
  98.4 10.5 %all_to_all.33 = f32[32,1,200]{2,1,0:T(1,128)S(1)} all-to-all(f32[32,1,200]{2,1,0:T(1,128)S(1)} %all_to_all.29), channel_id=1, replica_groups=mesh['tx'=2,'ty'=4,'gz'=4] {'tx','ty','gz'}, dimensions={0} | all-to-all | bytes 51200 | tf_op jit(solution)/shard_map/all_to_all | solution.py:200
  108.9 3.9 %all-to-all-start.1 = ((f32[100,16,128]{2,1,0:T(8,128)}), f32[100,16,128]{2,1,0:T(8,128)S(1)}, u32[]{:S(2)}, u32[]{:S(2)}) async-start(f32[100,16,128]{2,1,0:T(8,128)} %bitcast.3), calls=%async_computation.1 | async-start | bytes 1638400 | tf_op jit(solution)/shard_map/all_to_all | solution.py:197
  112.8 0.7 reshape.32
  113.5 10.4 %all-to-all-done.1 = f32[100,16,128]{2,1,0:T(8,128)S(1)} async-done(((f32[100,16,128]{2,1,0:T(8,128)}), f32[100,16,128]{2,1,0:T(8,128)S(1)}, u32[]{:S(2)}, u32[]{:S(2)}) %all-to-all-start.1) | async-done | bytes 819232 | tf_op jit(solution)/shard_map/all_to_all | solution.py:197
  123.9 1.0 copy.20
  (38 shorter events, 3.5 us)
Async XLA Ops:
  4.0 10.5 %copy-start.2 = (f32[3,64,128]{2,1,0:T(8,128)S(1)}, f32[3,64,128]{2,1,0:T(8,128)}, u32[]{:S(2)}) copy-start(f32[3,64,128]{2,1,0:T(8,128)} %param.9) | copy-start | bytes 294916
  4.4 5.8 %collective-permute-start = (f32[29,64,6]{1,0,2:T(8,128)S(1)}, f32[29,64,6]{1,0,2:T(8,128)S(1)}, u32[]{:S(2)}, u32[]{:S(2)}) collective-permute-start(f32[29,64,6]{1,0,2:T(8,128)S(1)} %copy.16), channel_id=1, source_target_pairs={{0,16},{1,17},{2,18},{3,19},{4,20},{5,21},{6,22},{7,23},{8,24},{9,... | collective-permute-start | bytes 133640 | tf_op jit(solution)/shard_map/ppermute | solution.py:17
  8.8 5.4 %collective-permute-start.1 = (f32[29,64,6]{1,0,2:T(8,128)S(1)}, f32[29,64,6]{1,0,2:T(8,128)S(1)}, u32[]{:S(2)}, u32[]{:S(2)}) collective-permute-start(f32[29,64,6]{1,0,2:T(8,128)S(1)} %copy.17), channel_id=1, source_target_pairs={{16,0},{17,1},{18,2},{19,3},{20,4},{21,5},{22,6},{23,7},{24,8},{25... | collective-permute-start | bytes 133640 | tf_op jit(solution)/shard_map/ppermute | solution.py:20
  10.6 8.7 %copy-start.1 = (f32[3,100]{1,0:T(4,128)S(1)}, f32[3,100]{1,0:T(4,128)}, u32[]{:S(2)}) copy-start(f32[3,100]{1,0:T(4,128)} %refs_0_.1) | copy-start | bytes 3604
  14.8 6.2 %collective-permute-start.2 = (f32[29,6,140]{2,1,0:T(8,128)S(1)}, f32[29,6,140]{2,1,0:T(8,128)S(1)}, u32[]{:S(2)}, u32[]{:S(2)}) collective-permute-start(f32[29,6,140]{2,1,0:T(8,128)S(1)} %get-tuple-element.6), channel_id=1, source_target_pairs={{0,4},{4,8},{8,12},{1,5},{5,9},{9,13},{2,6},{6,10},{10,14},{3,7},{... | collective-permute-start | bytes 292328 | tf_op jit(solution)/shard_map/ppermute | solution.py:17
  18.0 6.9 %collective-permute-start.3 = (f32[29,6,140]{2,1,0:T(8,128)S(1)}, f32[29,6,140]{2,1,0:T(8,128)S(1)}, u32[]{:S(2)}, u32[]{:S(2)}) collective-permute-start(f32[29,6,140]{2,1,0:T(8,128)S(1)} %get-tuple-element.7), channel_id=1, source_target_pairs={{4,0},{8,4},{12,8},{5,1},{9,5},{13,9},{6,2},{10,6},{14,10},{7,3},{... | collective-permute-start | bytes 292328 | tf_op jit(solution)/shard_map/ppermute | solution.py:20
  27.6 20.1 %copy-start.3 = (f32[100,100]{1,0:T(8,128)S(1)}, f32[100,100]{1,0:T(8,128)}, u32[]{:S(2)}) copy-start(f32[100,100]{1,0:T(8,128)} %param.12) | copy-start | bytes 120004
  27.6 20.2 %copy-start.4 = (s32[256]{0:T(256)S(1)}, s32[256]{0:T(256)}, u32[]{:S(2)}) copy-start(s32[256]{0:T(256)} %param.13) | copy-start | bytes 3076
  27.6 20.2 %copy-start.5 = (f32[256]{0:T(256)S(1)}, f32[256]{0:T(256)}, u32[]{:S(2)}) copy-start(f32[256]{0:T(256)} %param.15) | copy-start | bytes 3076
  27.6 20.2 %copy-start.6 = (s32[256]{0:T(256)S(1)}, s32[256]{0:T(256)}, u32[]{:S(2)}) copy-start(s32[256]{0:T(256)} %param.14) | copy-start | bytes 3076
  38.8 1.1 copy-start
  39.9 24.3 %all-to-all-start = ((f32[4,80,8,128]{3,2,1,0:T(8,128)}), f32[4,80,8,128]{3,2,1,0:T(8,128)}, u32[]{:S(2)}, u32[]{:S(2)}) async-start(f32[4,80,8,128]{3,2,1,0:T(8,128)} %copy-done), calls=%async_computation | async-start | bytes 2621440 | tf_op jit(solution)/shard_map/all_to_all | solution.py:182
  108.9 15.0 %all-to-all-start.1 = ((f32[100,16,128]{2,1,0:T(8,128)}), f32[100,16,128]{2,1,0:T(8,128)S(1)}, u32[]{:S(2)}, u32[]{:S(2)}) async-start(f32[100,16,128]{2,1,0:T(8,128)} %bitcast.3), calls=%async_computation.1 | async-start | bytes 1638400 | tf_op jit(solution)/shard_map/all_to_all | solution.py:197

commit v3 on v2

--- a/solution.py
+++ b/solution.py
@@ -21,10 +21,17 @@
     return jnp.concatenate([low, block, high], axis=dim)
 
 LANES = 128
+MESH = pl.DeviceIdType.MESH
 VMEM = pl.BlockSpec(memory_space=pltpu.VMEM)
 SMEM = pl.BlockSpec(memory_space=pltpu.SMEM)
 OFF = 4
 PARAMS = pltpu.CompilerParams(vmem_limit_bytes=48 * 1024 * 1024)
+
+
+def remote(number):
+    return pltpu.CompilerParams(
+        vmem_limit_bytes=48 * 1024 * 1024, collective_id=number, has_side_effects=True
+    )
 
 
 def substeps(a, wet, kx, ky, ks):
@@ -40,37 +47,114 @@
     return a
 
 
-def levels_kernel(local, parts, col_rows, base_ref, cv_ref, p_ref, out_ref, side):
+def greet(devices):
+    barrier = pltpu.get_barrier_semaphore()
+    for device in devices:
+        pl.semaphore_signal(barrier, inc=1, device_id=device, device_id_type=MESH)
+    pl.semaphore_wait(barrier, len(devices))
+
+
+def send(src, dst, sems, slot, own, device):
+    return pltpu.make_async_remote_copy(
+        src_ref=src, dst_ref=dst, send_sem=sems[0].at[slot], recv_sem=sems[1].at[own],
+        device_id=device, device_id_type=MESH,
+    )
+
+
+def levels_kernel(local, parts, col_rows, cv_ref, p_ref, out_ref, block, side, send_sem, recv_sem):
     tiles = (col_rows + 8) // 8
     coefs = [p_ref.at[local + c] for c in range(3)]
-
-    def level(l, carry):
-        k = (base_ref[0] + l).astype(jnp.float32)
-        wet = jnp.where(k < p_ref[local + 3], 1.0, 0.0)
-        a = substeps(p_ref[l], wet, *(c[...] * cv_ref[i, l] for i, c in enumerate(coefs)))
-        for part in range(parts):
-            for t in range(tiles):
-                row = part * col_rows + 8 * t
-                out_ref[part, tiles * l + t] = a[row : row + 8, :LANES]
-        side[l] = a[:, LANES:]
-        return carry
-
-    lax.fori_loop(0, local, level, 0)
+    me = lax.axis_index("gz")
+    tx, ty = lax.axis_index("tx"), lax.axis_index("ty")
+    peers = [lax.rem(me + d, parts) for d in range(1, parts)]
     lane = lax.broadcasted_iota(jnp.int32, (8, LANES), 1)
-
-    def pack(q, carry):
+    greet([(tx, ty, peer) for peer in peers])
+
+    def chunk(q, carry):
+        def level(j, carry):
+            l = 5 * q + j
+            k = (me * local + l).astype(jnp.float32)
+            wet = jnp.where(k < p_ref[local + 3], 1.0, 0.0)
+            a = substeps(p_ref[l], wet, *(c[...] * cv_ref[i, l] for i, c in enumerate(coefs)))
+            for part in range(parts):
+                for t in range(tiles):
+                    row = part * col_rows + 8 * t
+                    block[part, q, tiles * j + t] = a[row : row + 8, :LANES]
+            side[j] = a[:, LANES:]
+            return carry
+
+        lax.fori_loop(0, 5, level, 0)
         for part in range(parts):
             acc = jnp.zeros((8, LANES), jnp.float32)
             for j in range(5):
                 for t in range(tiles):
                     slot = 8 * (tiles * j + t)
                     row = part * col_rows + 8 * t
-                    tile = pltpu.roll(side[5 * q + j, row : row + 8, :], slot + NSUB, 1)
+                    tile = pltpu.roll(side[j, row : row + 8, :], slot + NSUB, 1)
                     acc = jnp.where((lane >= slot) & (lane < slot + 2 * NSUB), tile, acc)
-            out_ref[part, tiles * local + q] = acc
+            block[part, q, 5 * tiles] = acc
+        for peer in peers:
+            pltpu.make_async_remote_copy(
+                src_ref=block.at[peer, q], dst_ref=out_ref.at[me, q],
+                send_sem=send_sem.at[peer, q], recv_sem=recv_sem.at[me, q],
+                device_id=(tx, ty, peer), device_id_type=MESH,
+            ).start()
+        out_ref[me, q] = block[me, q]
         return carry
 
-    lax.fori_loop(0, local // 5, pack, 0)
+    chunks = local // 5
+    lax.fori_loop(0, chunks, chunk, 0)
+
+    def finish(q, carry):
+        for peer in peers:
+            pltpu.make_async_remote_copy(
+                src_ref=block.at[peer, q], dst_ref=out_ref.at[peer, q],
+                send_sem=send_sem.at[peer, q], recv_sem=recv_sem.at[peer, q],
+                device_id=(tx, ty, peer), device_id_type=MESH,
+            ).wait()
+        return carry
+
+    lax.fori_loop(0, chunks, finish, 0)
+
+
+def result_kernel(local, parts, col_rows, n_tx, n_ty, field_ref, flux_ref, out_ref, sum_ref,
+                  gates, part_flux, tile_flux, *sems):
+    me = lax.axis_index("gz")
+    tx, ty = lax.axis_index("tx"), lax.axis_index("ty")
+    tile, tiles = tx * n_ty + ty, n_tx * n_ty
+    peers = [lax.rem(me + d, parts) for d in range(1, parts)]
+    others = [lax.rem(tile + d, tiles) for d in range(1, tiles)]
+    rows = lambda at: pl.ds(pl.multiple_of(at * col_rows, col_rows), col_rows)
+    place = lambda peer: (tx, ty, peer)
+    owner = lambda other: (lax.div(other, n_ty), lax.rem(other, n_ty), me)
+    gate_rows = lambda at: pl.ds(pl.multiple_of(at * G_DEV, G_DEV), G_DEV)
+    greet([place(p) for p in peers] + [owner(o) for o in others])
+
+    def copies(kind, own, peer):
+        levels = pl.ds(peer * local, local)
+        if kind == 0:
+            return send(flux_ref.at[peer], part_flux.at[own], sems[0:2], peer, own, place(peer))
+        if kind == 1:
+            return send(field_ref.at[levels], out_ref.at[:, rows(own), :], sems[2:4], peer, own,
+                        place(peer))
+        return send(gates.at[gate_rows(peer)], tile_flux.at[own], sems[4:6], peer, own, owner(peer))
+
+    for kind in range(2):
+        for peer in peers:
+            copies(kind, me, peer).start()
+    out_ref[:, rows(me), :] = field_ref[pl.ds(me * local, local)]
+    part_flux[me] = flux_ref[me]
+    for peer in peers:
+        copies(0, peer, peer).wait()
+    gates[...] = jnp.sum(part_flux[...], axis=0)
+    for other in others:
+        copies(2, tile, other).start()
+    tile_flux[tile] = gates[gate_rows(tile)]
+    for other in others:
+        copies(2, other, other).wait()
+    sum_ref[...] = jnp.sum(tile_flux[...], axis=0)
+    for peer in peers:
+        copies(1, peer, peer).wait()
 
 
 def split(x):
@@ -88,23 +172,27 @@
 
     def unpack(q, carry):
         for part in range(parts):
-            packed = in_ref[part, tiles * local + q]
+            packed = in_ref[part, q, 5 * tiles]
             for j in range(5):
                 for t in range(tiles):
                     shift = LANES - NSUB - 8 * (tiles * j + t)
                     row = pl.multiple_of((part * local + 5 * q + j) * tall + 8 * t, 8)
                     side[pl.ds(row, 8), :] = jnp.where(rim, pltpu.roll(packed, shift, 1), 0.0)
-                    main[pl.ds(row, 8), :] = in_ref[part, tiles * (5 * q + j) + t]
+                    main[pl.ds(row, 8), :] = in_ref[part, q, tiles * j + t]
         return carry
 
     lax.fori_loop(0, local // 5, unpack, 0)
     inv_high, inv_low = split(inv_ref[...])
+    padded = inv_high.shape[0]
+    inv_both = jnp.concatenate([inv_high, inv_low], axis=0)
+    inv_high = inv_high[:levels]
     ids = lax.broadcasted_iota(jnp.int32, (levels, 2 * LANES), 0).astype(jnp.float32)
 
     def solve(field, bounds):
         high, low = split(field)
         dot = lambda a, b: jnp.dot(a, b, preferred_element_type=jnp.float32)
-        out = dot(inv_high, high) + (dot(inv_low, high) + dot(inv_high, low))
+        both = dot(inv_both, high)
+        out = both[:levels] + (both[padded : padded + levels] + dot(inv_high, low))
         return jnp.where(ids < bounds, out, 0.0)
 
     for r in range(1, tall - 1):
@@ -114,15 +202,17 @@
         main[at, :] = field[:, :LANES]
         side[at, :] = field[:, LANES:]
 
-    def level(k, carry):
-        at = pl.ds(pl.multiple_of(k * tall, 8), tall)
-        wet = jnp.where(k.astype(jnp.float32) < c_ref[3], 1.0, 0.0)
-        a = jnp.concatenate([main[at, :], side[at, :]], axis=1)
-        a = substeps(a, wet, *(c_ref[i] * cv_ref[i, k] for i in range(3)))
-        after[at, :] = a[:, :LANES]
+    def group(q, carry):
+        for j in range(4):
+            k = 4 * q + j
+            at = pl.ds(pl.multiple_of(k * tall, 8), tall)
+            wet = jnp.where(k.astype(jnp.float32) < c_ref[3], 1.0, 0.0)
+            a = jnp.concatenate([main[at, :], side[at, :]], axis=1)
+            a = substeps(a, wet, *(c_ref[i] * cv_ref[i, k] for i in range(3)))
+            after[at, :] = a[:, :LANES]
         return carry
 
-    lax.fori_loop(0, levels, level, 0)
+    lax.fori_loop(0, levels // 4, group, 0)
     flux = jnp.zeros(flux_ref.shape, jnp.float32)
     for r in range(0, col_rows, 2):
         ats = [pl.ds(OFF + r + i, levels, stride=tall) for i in range(2)]
@@ -130,11 +220,13 @@
         field = jnp.concatenate([after[at, :] for at in ats], axis=1)
         field = solve(field, jnp.concatenate(bounds, axis=1))
         for i in range(2):
-            half = field[:, i * LANES : (i + 1) * LANES]
-            out_ref[pl.ds(r + i, levels, stride=col_rows), :] = half
-            cells = m_ref[:, (r + i) * LANES : (r + i + 1) * LANES]
+            out_ref[pl.ds(r + i, levels, stride=col_rows), :] = field[:, i * LANES : (i + 1) * LANES]
+        first = jnp.concatenate([main[at, :] for at in ats], axis=1)
+        cells = split(m_ref[:, r * LANES : (r + 2) * LANES])
+        total = split(field + first)
+        for one, two in ((0, 0), (0, 1), (1, 0)):
             flux += lax.dot_general(
-                cells, half + main[ats[i], :], (((1,), (1,)), ((), ())), precision=HI,
+                cells[one], total[two], (((1,), (1,)), ((), ())),
                 preferred_element_type=jnp.float32,
             )
     flux_ref[...] = flux
@@ -148,6 +240,7 @@
     levels = local_levels * depth_count
     col_rows = rows // depth_count
     tall = col_rows + 8
+    chunks = local_levels // 5
     level_ids = depth_index * local_levels + jnp.arange(local_levels, dtype=jnp.int32)
     coef_depth = lax.dynamic_slice_in_dim(coef_v, depth_index * local_levels, local_levels, 1)
     row_start = depth_index * col_rows
@@ -170,16 +263,21 @@
     gap = jnp.zeros((channels, 2 * OFF + rows + 8 - packed.shape[1], 2 * LANES), jnp.float32)
     packed = jnp.concatenate([packed[:, rim - OFF :], gap, packed[:, : rim - OFF]], axis=1)
 
-    count = local_levels * tall // 8 + local_levels // 5
-    sent = pl.pallas_call(
+    blocks = (depth_count, chunks, 5 * tall // 8 + 1, 8, LANES)
+    dma = pltpu.SemaphoreType.DMA
+    got = pl.pallas_call(
         lambda *refs: levels_kernel(local_levels, depth_count, col_rows, *refs),
-        out_shape=jax.ShapeDtypeStruct((depth_count, count, 8, LANES), jnp.float32),
-        in_specs=[SMEM, SMEM, VMEM],
+        out_shape=jax.ShapeDtypeStruct(blocks, jnp.float32),
+        in_specs=[SMEM, VMEM],
         out_specs=VMEM,
-        scratch_shapes=[pltpu.VMEM((local_levels, packed.shape[1], LANES), jnp.float32)],
-        compiler_params=PARAMS,
-    )((depth_index * local_levels)[None].astype(jnp.int32), coef_depth, packed)
-    got = lax.all_to_all(sent, "gz", split_axis=0, concat_axis=0, tiled=True)
+        scratch_shapes=[
+            pltpu.VMEM(blocks, jnp.float32),
+            pltpu.VMEM((5, packed.shape[1], LANES), jnp.float32),
+            dma((depth_count, chunks)),
+            dma((depth_count, chunks)),
+        ],
+        compiler_params=remote(0),
+    )(coef_depth, packed)
 
     window = lax.dynamic_slice_in_dim(packed[local_levels:], row_start, tall, 1)
     field, flux = pl.pallas_call(
@@ -192,13 +290,30 @@
         out_specs=(VMEM, VMEM),
         scratch_shapes=[pltpu.VMEM((levels * tall, LANES), jnp.float32)] * 3,
         compiler_params=PARAMS,
-    )(coef_v, column_inv.T, window, gate_cells, got)
+    )(coef_v, jnp.pad(column_inv.T, ((0, -levels % 16), (0, 0))), window, gate_cells, got)
     field = field.reshape(levels, col_rows, width)
-    out = lax.all_to_all(field, "gz", split_axis=0, concat_axis=1, tiled=True)
-    flux = flux.reshape(tiles, G_DEV, depth_count, local_levels).transpose(0, 2, 1, 3)
-    flux = flux.reshape(tiles * depth_count, G_DEV * local_levels)
-    flux = lax.all_to_all(flux, ("tx", "ty", "gz"), split_axis=0, concat_axis=0, tiled=True)
-    flux = jnp.sum(flux, axis=0).reshape(G_DEV, local_levels)
+    flux = flux.reshape(-1, depth_count, local_levels).transpose(1, 0, 2)
+    flux = jnp.pad(flux, ((0, 0), (0, 0), (0, LANES - local_levels)))
+    out, flux = pl.pallas_call(
+        lambda *refs: result_kernel(
+            local_levels, depth_count, col_rows, lax.axis_size("tx"), lax.axis_size("ty"), *refs
+        ),
+        out_shape=(
+            jax.ShapeDtypeStruct((local_levels, rows, width), jnp.float32),
+            jax.ShapeDtypeStruct((G_DEV, LANES), jnp.float32),
+        ),
+        in_specs=[VMEM, VMEM],
+        out_specs=(VMEM, VMEM),
+        scratch_shapes=[
+            pltpu.VMEM((G_DEV * tiles, LANES), jnp.float32),
+            pltpu.VMEM((depth_count, G_DEV * tiles, LANES), jnp.float32),
+            pltpu.VMEM((tiles, G_DEV, LANES), jnp.float32),
+        ]
+        + [dma((depth_count,))] * 4
+        + [dma((tiles,))] * 2,
+        compiler_params=remote(1),
+    )(field, flux)
+    flux = flux[:, :local_levels]
     return (out, flux)
 
 

time: 126 us -> 81.7 us (0.65)
  waiting for transfers between devices: 34.8 us -> 8 us
  starting transfers between devices: 21.4 us -> 9.77 us
  blocking collectives: 10.5 us -> 0 us
  Pallas kernels: 45.2 us -> 50.9 us
    all_to_all x2 -> x0, waiting for transfers between devices: 25.8 us -> none  [the longest x1 15.4 us: per_device(): got = lax.all_to_all(sent, 'gz', split_axis=0, concat_axis=0, tiled=True)]
    pallas_call x1, Pallas kernels: 33.9 us -> 12.8 us  [per_device(): pl.pallas_call(lambda *refs: columns_kernel(local_levels, depth_count, co...]
    pallas_call x0 -> x1, Pallas kernels: none -> 15.1 us  [per_device(): pl.pallas_call(lambda *refs: result_kernel(local_levels, depth_count, col...]
    pallas_call x1, Pallas kernels: 11.2 us -> 23 us  [per_device(): pl.pallas_call(lambda *refs: levels_kernel(local_levels, depth_count, col...]
    all_to_all x2 -> x0, starting transfers between devices: 11.6 us -> none  [the longest x1 7.78 us: per_device(): got = lax.all_to_all(sent, 'gz', split_axis=0, concat_axis=0, tiled=True)]
    all_to_all x1 -> x0, blocking collectives: 10.5 us -> none  [per_device(): lax.all_to_all(flux, ('tx', 'ty', 'gz'), split_axis=0, concat_axis=0, til...]
  transfers between devices with their start and end apart: 6 -> 4, of which waited for: 5 -> 3; matrix products, arithmetic and copies ran while one was open for 2% -> 2% of each run, Pallas kernels for 0% -> 0%
where the time goes in v3:
time: 81.7 us; the launch traced here: 81.3 us
  Pallas kernels  50.9 us (62%)
  starting transfers between devices  9.77 us (12%)
  waiting for transfers between devices  8 us (10%)
  local copies, waits for them, and re-layouts  5.8 us (7%)
  other arithmetic  4.98 us (6%)
  between operations  0.93 us (1%)
  matrix products  0.91 us (1%)
    pallas_call x1, Pallas kernels, per_device(): pl.pallas_call(lambda *refs: levels_kernel(local_levels, depth_count, col...  23 us
    pallas_call x1, Pallas kernels, per_device(): pl.pallas_call(lambda *refs: result_kernel(local_levels, depth_count, col...  15.1 us
    pallas_call x1, Pallas kernels, per_device(): pl.pallas_call(lambda *refs: columns_kernel(local_levels, depth_count, co...  12.8 us
    ppermute x2, starting transfers between devices, extended(): lax.ppermute(lax.slice_in_dim(block, block.shape[dim] - width, None, axis...  7.19 us
    ppermute x2, waiting for transfers between devices, extended(): lax.ppermute(lax.slice_in_dim(block, 0, width, axis=dim), axis, backward)  6.36 us
    ppermute x2, starting transfers between devices, extended(): lax.ppermute(lax.slice_in_dim(block, 0, width, axis=dim), axis, backward)  2.58 us
    ppermute x2, waiting for transfers between devices, extended(): lax.ppermute(lax.slice_in_dim(block, block.shape[dim] - width, None, axis...  1.64 us
  transfers between devices with their start and end apart: 4, of which 3 were waited for; matrix products, arithmetic and copies ran while one was open for 2% of the time, Pallas kernels for 0%

profile of v3, /device:TPU:1, one launch (start us, length us, event | category | flops | bytes accessed | tf_op | source)
XLA Modules:
  0.0 81.3 jit_solution(17057053183630729174)
XLA Ops:
  0.6 0.8 convert_bitcast_fusion
  1.4 1.3 %compare_select_fusion = f32[25,64,128]{2,1,0:T(8,128)S(1)} fusion(f32[25,64,128]{2,1,0:T(8,128)} %param.8, s32[64,128]{1,0:T(8,128)} %param.11, s32[25]{0:T(128)S(1)} %iota_add_fusion.1), kind=kLoop, calls=%fused_computation.8 | loop fusion | flops 409600 | bytes 1671268 | tf_op jit(solution)/shard_map/mul | solution.py:257
  2.7 1.0 %pad_maximum_fusion.3 = f32[29,64,128]{2,1,0:T(8,128)S(1)} fusion(f32[1,64,128]{2,1,0:T(8,128)S(1)} %convert_bitcast_fusion, f32[3,64,128]{2,1,0:T(8,128)} %param.9, f32[25,64,128]{2,1,0:T(8,128)S(1)} %compare_select_fusion), kind=kLoop, calls=%fused_computation.7 | loop fusion | flops 475136 | bytes 1900544 | tf_op jit(solution)/shard_map/concatenate | solution.py:256
  4.0 0.4 copy.15
  4.4 4.0 %collective-permute-start = (f32[29,64,6]{1,0,2:T(8,128)S(1)}, f32[29,64,6]{1,0,2:T(8,128)S(1)}, u32[]{:S(2)}, u32[]{:S(2)}) collective-permute-start(f32[29,64,6]{1,0,2:T(8,128)S(1)} %copy.15), channel_id=1, source_target_pairs={{0,16},{1,17},{2,18},{3,19},{4,20},{5,21},{6,22},{7,23},{8,24},{9,... | collective-permute-start | bytes 133640 | tf_op jit(solution)/shard_map/ppermute | solution.py:17
  8.4 0.4 copy.16
  8.8 1.3 %collective-permute-start.1 = (f32[29,64,6]{1,0,2:T(8,128)S(1)}, f32[29,64,6]{1,0,2:T(8,128)}, u32[]{:S(2)}, u32[]{:S(2)}) collective-permute-start(f32[29,64,6]{1,0,2:T(8,128)S(1)} %copy.16), channel_id=1, source_target_pairs={{16,0},{17,1},{18,2},{19,3},{20,4},{21,5},{22,6},{23,7},{24,8},{25... | collective-permute-start | bytes 133640 | tf_op jit(solution)/shard_map/ppermute | solution.py:20
  10.1 0.9 %fusion.refs_3_ = f32[64,2048]{1,0:T(8,128)S(1)} fusion(s32[2048]{0:T(1024)S(1)} %iota_add_fusion, s32[256]{0:T(256)S(1)} %copy-done.3, f32[256]{0:T(256)S(1)} %copy-done.4, s32[256]{0:T(256)S(1)} %copy-done.5), kind=kOutput, calls=%fused_computation.3 | convolution fusion | flops 403210240 | bytes 535552 | tf_op jit(solution)/shard_map/dot_general | solution.py:252
  11.3 0.4 copy.17
  11.7 2.5 %collective-permute-done.1 = f32[29,64,6]{1,0,2:T(8,128)} collective-permute-done((f32[29,64,6]{1,0,2:T(8,128)S(1)}, f32[29,64,6]{1,0,2:T(8,128)}, u32[]{:S(2)}, u32[]{:S(2)}) %collective-permute-start.1) | collective-permute-done | bytes 44576 | tf_op jit(solution)/shard_map/ppermute | solution.py:20
  14.3 1.3 %copy.18 = f32[29,64,6]{2,1,0:T(8,128)S(1)} copy(f32[29,64,6]{1,0,2:T(8,128)} %collective-permute-done.1) | data formatting | bytes 89088 | tf_op jit(solution)/shard_map/ppermute | solution.py:20
  15.8 3.2 %collective-permute-start.2 = (f32[29,6,140]{2,1,0:T(8,128)S(1)}, f32[29,6,140]{2,1,0:T(8,128)S(1)}, u32[]{:S(2)}, u32[]{:S(2)}) collective-permute-start(f32[29,6,140]{2,1,0:T(8,128)S(1)} %get-tuple-element.10), channel_id=1, source_target_pairs={{0,4},{4,8},{8,12},{1,5},{5,9},{9,13},{2,6},{6,10},{10,14},{3,7},{... | collective-permute-start | bytes 292328 | tf_op jit(solution)/shard_map/ppermute | solution.py:17
  19.0 1.3 %collective-permute-start.3 = (f32[29,6,140]{2,1,0:T(8,128)S(1)}, f32[29,6,140]{2,1,0:T(8,128)S(1)}, u32[]{:S(2)}, u32[]{:S(2)}) collective-permute-start(f32[29,6,140]{2,1,0:T(8,128)S(1)} %get-tuple-element.11), channel_id=1, source_target_pairs={{4,0},{8,4},{12,8},{5,1},{9,5},{13,9},{6,2},{10,6},{14,10},{7,3},{... | collective-permute-start | bytes 292328 | tf_op jit(solution)/shard_map/ppermute | solution.py:20
  20.4 1.6 %collective-permute-done.2 = f32[29,6,140]{2,1,0:T(8,128)S(1)} collective-permute-done((f32[29,6,140]{2,1,0:T(8,128)S(1)}, f32[29,6,140]{2,1,0:T(8,128)S(1)}, u32[]{:S(2)}, u32[]{:S(2)}) %collective-permute-start.2) | collective-permute-done | bytes 97472 | tf_op jit(solution)/shard_map/ppermute | solution.py:17
  22.0 3.8 %collective-permute-done.3 = f32[29,6,140]{2,1,0:T(8,128)S(1)} collective-permute-done((f32[29,6,140]{2,1,0:T(8,128)S(1)}, f32[29,6,140]{2,1,0:T(8,128)S(1)}, u32[]{:S(2)}, u32[]{:S(2)}) %collective-permute-start.3) | collective-permute-done | bytes 97472 | tf_op jit(solution)/shard_map/ppermute | solution.py:20
  25.9 0.9 %pad_maximum_fusion = f32[29,76,140]{2,1,0:T(8,128)S(1)} fusion(f32[29,6,140]{2,1,0:T(8,128)S(1)} %collective-permute-done.3, f32[29,64,6]{2,1,0:T(8,128)S(1)} %copy.18, f32[1,64,128]{2,1,0:T(8,128)S(1)} %convert_bitcast_fusion, f32[3,64,128]{2,1,0:T(8,128)S(1)} %copy-done.1, f32[25,64,128]{2,1,0:T(8,128)S(1)} %compare_select_fusion, ...), kind=kLoop, calls=%fused_computation | loop fusion | flops 1851360 | bytes 2468480 | tf_op jit(solution)/shard_map/concatenate | solution.py:21
  26.8 0.7 slice.42
  27.6 0.4 pad_maximum_fusion.1
  28.3 0.4 pad_maximum_fusion.2.refs_1_
  28.7 23.0 %shard_map.95.refs_4_ = f32[4,5,16,8,128]{4,3,2,1,0:T(8,128)S(1)} custom-call(f32[3,25]{1,0:T(4,128)S(1)} %constant_dynamic-slice_fusion.refs_0_, f32[29,80,256]{2,1,0:T(8,128)S(1)} %pad_maximum_fusion.2.refs_1_), custom_call_target="tpu_custom_call" | custom-call | tf_op jit(solution)/shard_map/pallas_call | solution.py:268
  51.7 12.8 %shard_map.96 = (f32[1600,128]{1,0:T(8,128)S(1)}, f32[64,100]{1,0:T(8,128)S(1)}) custom-call(f32[3,100]{1,0:T(4,128)S(1)} %copy-done, f32[112,100]{1,0:T(8,128)S(1)} %pad.8.refs_1_, f32[4,24,256]{2,1,0:T(8,128)S(1)} %constant_dynamic-slice_fusion.1.refs_2_, f32[64,2048]{1,0:T(8,128)S(1)} %fusion.refs_3_, f32[4,5,16,8,128]{4,3,2,1,0:T(8,128)S(1)} %shard_map.95.refs_4_), custom_call_target="tpu_custom_call" | custom-call | tf_op jit(solution)/shard_map/pallas_call | solution.py:283
  64.7 15.1 %shard_map.97 = (f32[25,64,128]{2,1,0:T(8,128)S(1)}, f32[8,128]{1,0:T(8,128)S(1)}) custom-call(f32[100,16,128]{2,1,0:T(8,128)S(1)} %bitcast.8, f32[4,64,128]{2,1,0:T(8,128)S(1)} %pad.9.refs_1_), custom_call_target="tpu_custom_call" | custom-call | tf_op jit(solution)/shard_map/pallas_call | solution.py:297
  79.8 0.9 %copy.27 = f32[25,64,128]{2,1,0:T(8,128)} copy(f32[25,64,128]{2,1,0:T(8,128)S(1)} %get-tuple-element.16) | data formatting | bytes 1638400
  80.7 0.6 copy.28
  (32 shorter events, 1.5 us)
Async XLA Ops:
  3.6 6.5 %copy-start.3 = (s32[256]{0:T(256)S(1)}, s32[256]{0:T(256)}, u32[]{:S(2)}) copy-start(s32[256]{0:T(256)} %param.13) | copy-start | bytes 3076
  3.7 6.5 %copy-start.4 = (f32[256]{0:T(256)S(1)}, f32[256]{0:T(256)}, u32[]{:S(2)}) copy-start(f32[256]{0:T(256)} %param.15) | copy-start | bytes 3076
  3.7 6.5 %copy-start.5 = (s32[256]{0:T(256)S(1)}, s32[256]{0:T(256)}, u32[]{:S(2)}) copy-start(s32[256]{0:T(256)} %param.14) | copy-start | bytes 3076
  3.7 7.5 %copy-start.2 = (f32[100,100]{1,0:T(8,128)S(1)}, f32[100,100]{1,0:T(8,128)}, u32[]{:S(2)}) copy-start(f32[100,100]{1,0:T(8,128)} %param.12) | copy-start | bytes 120004
  4.0 11.5 %copy-start.1 = (f32[3,64,128]{2,1,0:T(8,128)S(1)}, f32[3,64,128]{2,1,0:T(8,128)}, u32[]{:S(2)}) copy-start(f32[3,64,128]{2,1,0:T(8,128)} %param.9) | copy-start | bytes 294916
  4.4 6.9 %collective-permute-start = (f32[29,64,6]{1,0,2:T(8,128)S(1)}, f32[29,64,6]{1,0,2:T(8,128)S(1)}, u32[]{:S(2)}, u32[]{:S(2)}) collective-permute-start(f32[29,64,6]{1,0,2:T(8,128)S(1)} %copy.15), channel_id=1, source_target_pairs={{0,16},{1,17},{2,18},{3,19},{4,20},{5,21},{6,22},{7,23},{8,24},{9,... | collective-permute-start | bytes 133640 | tf_op jit(solution)/shard_map/ppermute | solution.py:17
  8.8 5.5 %collective-permute-start.1 = (f32[29,64,6]{1,0,2:T(8,128)S(1)}, f32[29,64,6]{1,0,2:T(8,128)}, u32[]{:S(2)}, u32[]{:S(2)}) collective-permute-start(f32[29,64,6]{1,0,2:T(8,128)S(1)} %copy.16), channel_id=1, source_target_pairs={{16,0},{17,1},{18,2},{19,3},{20,4},{21,5},{22,6},{23,7},{24,8},{25... | collective-permute-start | bytes 133640 | tf_op jit(solution)/shard_map/ppermute | solution.py:20
  11.7 8.6 %copy-start = (f32[3,100]{1,0:T(4,128)S(1)}, f32[3,100]{1,0:T(4,128)}, u32[]{:S(2)}) copy-start(f32[3,100]{1,0:T(4,128)} %refs_0_.1) | copy-start | bytes 3604
  15.8 6.2 %collective-permute-start.2 = (f32[29,6,140]{2,1,0:T(8,128)S(1)}, f32[29,6,140]{2,1,0:T(8,128)S(1)}, u32[]{:S(2)}, u32[]{:S(2)}) collective-permute-start(f32[29,6,140]{2,1,0:T(8,128)S(1)} %get-tuple-element.10), channel_id=1, source_target_pairs={{0,4},{4,8},{8,12},{1,5},{5,9},{9,13},{2,6},{6,10},{10,14},{3,7},{... | collective-permute-start | bytes 292328 | tf_op jit(solution)/shard_map/ppermute | solution.py:17
  19.0 6.9 %collective-permute-start.3 = (f32[29,6,140]{2,1,0:T(8,128)S(1)}, f32[29,6,140]{2,1,0:T(8,128)S(1)}, u32[]{:S(2)}, u32[]{:S(2)}) collective-permute-start(f32[29,6,140]{2,1,0:T(8,128)S(1)} %get-tuple-element.11), channel_id=1, source_target_pairs={{4,0},{8,4},{12,8},{5,1},{9,5},{13,9},{6,2},{10,6},{14,10},{7,3},{... | collective-permute-start | bytes 292328 | tf_op jit(solution)/shard_map/ppermute | solution.py:20

commit v4 on v3

--- a/solution.py
+++ b/solution.py
@@ -9,16 +9,6 @@
 G_DEV = 8
 HI = lax.Precision.HIGHEST
 
-
-def extended(block, axis, dim, width):
-    count = lax.axis_size(axis)
-    forward = [(i, i + 1) for i in range(count - 1)]
-    backward = [(target, source) for source, target in forward]
-    low = lax.ppermute(
-        lax.slice_in_dim(block, block.shape[dim] - width, None, axis=dim), axis, forward
-    )
-    high = lax.ppermute(lax.slice_in_dim(block, 0, width, axis=dim), axis, backward)
-    return jnp.concatenate([low, block, high], axis=dim)
 
 LANES = 128
 MESH = pl.DeviceIdType.MESH
@@ -61,21 +51,133 @@
     )
 
 
-def levels_kernel(local, parts, col_rows, cv_ref, p_ref, out_ref, block, side, send_sem, recv_sem):
+def exchange_rims(n_tx, n_ty, tracer_ref, coef_ref, wet_ref, p_ref, x_sent, x_got, sems):
+    tx, ty, me = lax.axis_index("tx"), lax.axis_index("ty"), lax.axis_index("gz")
+    local, rows, _ = tracer_ref.shape
+    wide = 2 * NSUB
+    pairs = p_ref.shape[0] // 2
+    lane = lax.broadcasted_iota(jnp.int32, (8, LANES), 1)
+    has_next = (tx < n_tx - 1, ty < n_ty - 1)
+    has_prior = (tx > 0, ty > 0)
+
+    def fill(l, carry):
+        p_ref[l, :rows, :LANES] = tracer_ref[l]
+        return carry
+
+    lax.fori_loop(0, local, fill, 0)
+    for c in range(3):
+        p_ref[local + c, :rows, :LANES] = coef_ref[c]
+    p_ref[local + 3, :rows, :LANES] = wet_ref[...].astype(jnp.float32)
+    for c in range(local + 4, p_ref.shape[0]):
+        p_ref[c, :rows, :LANES] = jnp.zeros((rows, LANES), jnp.float32)
+
+    def copy(kind, way):
+        step = 1 - 2 * way
+        if kind == 0:
+            src, dst, device = x_sent.at[way], x_got.at[way], (tx + step, ty, me)
+        else:
+            half = pl.ds((kind - 1) * LANES, LANES)
+            src = p_ref.at[:, pl.ds((rows - 8) * (1 - way), 8), half]
+            dst = p_ref.at[:, pl.ds(rows + 8 * (1 - way), 8), half]
+            device = (tx, ty + step, me)
+        return pltpu.make_async_remote_copy(
+            src_ref=src, dst_ref=dst, send_sem=sems[0].at[kind, way],
+            recv_sem=sems[1].at[kind, way], device_id=device, device_id_type=MESH,
+        )
+
+    def start(kind):
+        axis = min(kind, 1)
+        for way, there in enumerate((has_next[axis], has_prior[axis])):
+            pl.when(there)(lambda way=way: copy(kind, way).start())
+
+    def wait(kind):
+        axis = min(kind, 1)
+        for way in range(2):
+            to, source = (has_next[axis], has_prior[axis])[:: 1 - 2 * way]
+            pl.when(to)(lambda way=way: copy(kind, way).wait_send())
+            pl.when(source)(lambda way=way: copy(kind, way).wait_recv())
+
+    def turn(tile, shift):
+        return pltpu.roll(tile, shift % LANES, 1) if shift % LANES else tile
+
+    start(1)
+
+    def pack(q, carry):
+        east = west = jnp.zeros((8, LANES), jnp.float32)
+        for j in range(2):
+            for t in range(8):
+                slot = 8 * (8 * j + t)
+                tile = p_ref[2 * q + j, 8 * t : 8 * t + 8, :LANES]
+                mask = (lane >= slot) & (lane < slot + wide)
+                east = jnp.where(mask, turn(tile, slot + wide), east)
+                west = jnp.where(mask, turn(tile, slot), west)
+        x_sent[0, q] = east
+        x_sent[1, q] = west
+        return carry
+
+    lax.fori_loop(0, pairs, pack, 0)
+    start(0)
+
+    @pl.when(jnp.logical_not(has_prior[0]))
+    def _():
+        x_got[0] = jnp.zeros(x_got.shape[1:], jnp.float32)
+
+    @pl.when(jnp.logical_not(has_next[0]))
+    def _():
+        x_got[1] = jnp.zeros(x_got.shape[1:], jnp.float32)
+
+    edge = jnp.zeros((p_ref.shape[0], 8, 2 * LANES), jnp.float32)
+
+    @pl.when(jnp.logical_not(has_prior[1]))
+    def _():
+        p_ref[:, rows + 8 : rows + 16, :] = edge
+
+    @pl.when(jnp.logical_not(has_next[1]))
+    def _():
+        p_ref[:, rows : rows + 8, :] = edge
+
+    wait(0)
+
+    def unpack(q, carry):
+        low, high = x_got[0, q], x_got[1, q]
+        for j in range(2):
+            for t in range(8):
+                slot = 8 * (8 * j + t)
+                tile = jnp.where(lane >= LANES - wide, turn(low, -slot - wide), 0.0)
+                tile = jnp.where(lane < wide, turn(high, -slot), tile)
+                p_ref[2 * q + j, 8 * t : 8 * t + 8, LANES:] = tile
+        return carry
+
+    lax.fori_loop(0, pairs, unpack, 0)
+    start(2)
+    wait(1)
+    wait(2)
+
+
+def levels_kernel(local, parts, col_rows, n_tx, n_ty, cv_ref, tracer_ref, coef_ref, wet_ref,
+                  out_ref, window_ref, p_ref, x_sent, x_got, turned, block, side,
+                  rim_send, rim_recv, send_sem, recv_sem):
     tiles = (col_rows + 8) // 8
     coefs = [p_ref.at[local + c] for c in range(3)]
     me = lax.axis_index("gz")
     tx, ty = lax.axis_index("tx"), lax.axis_index("ty")
     peers = [lax.rem(me + d, parts) for d in range(1, parts)]
     lane = lax.broadcasted_iota(jnp.int32, (8, LANES), 1)
-    greet([(tx, ty, peer) for peer in peers])
+    around = [(lax.rem(tx + d, n_tx), ty, me) for d in (1, n_tx - 1)]
+    around += [(tx, lax.rem(ty + d, n_ty), me) for d in (1, n_ty - 1)]
+    greet([(tx, ty, peer) for peer in peers] + around)
+    exchange_rims(
+        n_tx, n_ty, tracer_ref, coef_ref, wet_ref, p_ref, x_sent, x_got, (rim_send, rim_recv)
+    )
 
     def chunk(q, carry):
         def level(j, carry):
             l = 5 * q + j
             k = (me * local + l).astype(jnp.float32)
             wet = jnp.where(k < p_ref[local + 3], 1.0, 0.0)
-            a = substeps(p_ref[l], wet, *(c[...] * cv_ref[i, l] for i, c in enumerate(coefs)))
+            a = wet * p_ref[l]
+            a = substeps(a, wet, *(c[...] * cv_ref[i, l] for i, c in enumerate(coefs)))
+            a = pltpu.roll(a, OFF, 0)
             for part in range(parts):
                 for t in range(tiles):
                     row = part * col_rows + 8 * t
@@ -104,6 +206,10 @@
 
     chunks = local // 5
     lax.fori_loop(0, chunks, chunk, 0)
+    own = pl.ds(pl.multiple_of(me * col_rows, 8), col_rows + 8)
+    for c in range(4):
+        turned[...] = pltpu.roll(p_ref[local + c], OFF, 0)
+        window_ref[c] = turned[own, :]
 
     def finish(q, carry):
         for peer in peers:
@@ -241,7 +347,6 @@
     col_rows = rows // depth_count
     tall = col_rows + 8
     chunks = local_levels // 5
-    level_ids = depth_index * local_levels + jnp.arange(local_levels, dtype=jnp.int32)
     coef_depth = lax.dynamic_slice_in_dim(coef_v, depth_index * local_levels, local_levels, 1)
     row_start = depth_index * col_rows
 
@@ -251,35 +356,34 @@
     cell_hot = (sec_cell[:, None] == cells[None, :]).astype(jnp.float32)
     gate_cells = jnp.dot(gate_hot, cell_hot, precision=HI)
 
-    rim = 2 * NSUB
-    wet_depth = (level_ids[:, None, None] < wet_levels[None]).astype(jnp.float32)
-    packed = jnp.concatenate(
-        [wet_depth * tracer_in, coef_h, wet_levels[None].astype(jnp.float32)], axis=0
-    )
-    packed = extended(extended(packed, "tx", 2, rim), "ty", 1, rim)
-    channels = packed.shape[0]
-    gap = jnp.zeros((channels, packed.shape[1], 2 * LANES - packed.shape[2]), jnp.float32)
-    packed = jnp.concatenate([packed[:, :, rim:], gap, packed[:, :, :rim]], axis=2)
-    gap = jnp.zeros((channels, 2 * OFF + rows + 8 - packed.shape[1], 2 * LANES), jnp.float32)
-    packed = jnp.concatenate([packed[:, rim - OFF :], gap, packed[:, : rim - OFF]], axis=1)
-
+    channels = local_levels + 4 + (local_levels + 4) % 2
     blocks = (depth_count, chunks, 5 * tall // 8 + 1, 8, LANES)
     dma = pltpu.SemaphoreType.DMA
-    got = pl.pallas_call(
-        lambda *refs: levels_kernel(local_levels, depth_count, col_rows, *refs),
-        out_shape=jax.ShapeDtypeStruct(blocks, jnp.float32),
-        in_specs=[SMEM, VMEM],
-        out_specs=VMEM,
+    got, window = pl.pallas_call(
+        lambda *refs: levels_kernel(
+            local_levels, depth_count, col_rows, lax.axis_size("tx"), lax.axis_size("ty"), *refs
+        ),
+        out_shape=(
+            jax.ShapeDtypeStruct(blocks, jnp.float32),
+            jax.ShapeDtypeStruct((4, tall, 2 * LANES), jnp.float32),
+        ),
+        in_specs=[SMEM, VMEM, VMEM, VMEM],
+        out_specs=(VMEM, VMEM),
         scratch_shapes=[
+            pltpu.VMEM((channels, rows + 16, 2 * LANES), jnp.float32),
+            pltpu.VMEM((2, channels // 2, 8, LANES), jnp.float32),
+            pltpu.VMEM((2, channels // 2, 8, LANES), jnp.float32),
+            pltpu.VMEM((rows + 16, 2 * LANES), jnp.float32),
             pltpu.VMEM(blocks, jnp.float32),
-            pltpu.VMEM((5, packed.shape[1], LANES), jnp.float32),
+            pltpu.VMEM((5, rows + 16, LANES), jnp.float32),
+            dma((3, 2)),
+            dma((3, 2)),
             dma((depth_count, chunks)),
             dma((depth_count, chunks)),
         ],
         compiler_params=remote(0),
-    )(coef_depth, packed)
-
-    window = lax.dynamic_slice_in_dim(packed[local_levels:], row_start, tall, 1)
+    )(coef_depth, tracer_in, coef_h, wet_levels)
+
     field, flux = pl.pallas_call(
         lambda *refs: columns_kernel(local_levels, depth_count, col_rows, *refs),
         out_shape=(

time: 81.7 us -> 67.7 us (0.83)
  starting transfers between devices: 9.77 us -> 0 us
  Pallas kernels: 50.9 us -> 60 us
  waiting for transfers between devices: 8 us -> 0 us
  other arithmetic: 4.98 us -> 0.01 us
    ppermute x4 -> x0, starting transfers between devices: 9.77 us -> none  [the longest x2 7.19 us: extended(): lax.ppermute(lax.slice_in_dim(block, block.shape[dim] - width, None, axis...]
    pallas_call x1, Pallas kernels: 23 us -> 32.4 us  [per_device(): pl.pallas_call(lambda *refs: levels_kernel(local_levels, depth_count, col...]
    ppermute x4 -> x0, waiting for transfers between devices: 8 us -> none  [the longest x2 6.36 us: extended(): lax.ppermute(lax.slice_in_dim(block, 0, width, axis=dim), axis, backward)]
    concatenate x4 -> x0, other arithmetic: 2.69 us -> none  [the longest x1 0.96 us: per_device(): jnp.concatenate([wet_depth * tracer_in, coef_h, wet_levels[None].astype(j...]
    unnamed x15 -> x11, local copies, waits for them, and re-layouts: 1.62 us -> 4.04 us
    slice x8 -> x0, local copies, waits for them, and re-layouts: 2.12 us -> none  [the longest x2 0.72 us: extended(): lax.slice_in_dim(block, block.shape[dim] - width, None, axis=dim)]
    ppermute x2 -> x0, local copies, waits for them, and re-layouts: 1.63 us -> none  [the longest x1 1.26 us: extended(): lax.ppermute(lax.slice_in_dim(block, 0, width, axis=dim), axis, backward)]
    mul x1 -> x0, other arithmetic: 1.27 us -> none  [per_device(): wet_depth * tracer_in]
  transfers between devices with their start and end apart: 4 -> 0, of which waited for: 3 -> 0; matrix products, arithmetic and copies ran while one was open for 2% -> 0% of each run, Pallas kernels for 0% -> 0%
where the time goes in v4:
time: 67.7 us; the launch traced here: 67.4 us
  Pallas kernels  60 us (89%)
  local copies, waits for them, and re-layouts  5.05 us (7%)
  matrix products  1.62 us (2%)
  between operations  0.72 us (1%)
    pallas_call x1, Pallas kernels, per_device(): pl.pallas_call(lambda *refs: levels_kernel(local_levels, depth_count, col...  32.4 us
    pallas_call x1, Pallas kernels, per_device(): pl.pallas_call(lambda *refs: result_kernel(local_levels, depth_count, col...  14.7 us
    pallas_call x1, Pallas kernels, per_device(): pl.pallas_call(lambda *refs: columns_kernel(local_levels, depth_count, co...  12.9 us
    unnamed x11, local copies, waits for them, and re-layouts  4.04 us
    dot_general x1, matrix products, per_device(): gate_cells = jnp.dot(gate_hot, cell_hot, precision=HI)  1.62 us

profile of v4, /device:TPU:1, one launch (start us, length us, event | category | flops | bytes accessed | tf_op | source)
XLA Modules:
  0.0 67.4 jit_solution(15046556914911006327)
XLA Ops:
  0.6 0.0 copy-start.3
  0.6 0.0 copy-start
  0.7 0.8 %constant_dynamic-slice_fusion.refs_0_ = f32[3,25]{1,0:T(4,128)S(1)} fusion(f32[3,100]{1,0:T(4,128)} %refs_0_.1, s32[]{:T(128)S(6)} %select_n.7), kind=kLoop, calls=%fused_computation.11 | loop fusion | bytes 604 | tf_op jit(solution)/shard_map/dynamic_slice | solution.py:350
  1.5 0.9 %copy.11 = f32[100,100]{0,1:T(8,128)S(1)} copy(f32[100,100]{1,0:T(8,128)} %param.12) | data formatting | bytes 80000 | tf_op args[4]
  2.4 1.6 %fusion.refs_3_ = f32[64,2048]{1,0:T(8,128)S(1)} fusion(s32[2048]{0:T(1024)S(1)} %iota_add_fusion, s32[256]{0:T(256)} %param.13, f32[256]{0:T(256)} %param.15, s32[256]{0:T(256)} %param.14), kind=kOutput, calls=%fused_computation | convolution fusion | flops 403210240 | bytes 535552 | tf_op jit(solution)/shard_map/dot_general | solution.py:357
  4.0 0.0 copy-done
  4.0 0.0 copy-start.1
  4.1 0.9 %copy-done.1 = f32[3,64,128]{2,1,0:T(8,128)S(1)} copy-done((f32[3,64,128]{2,1,0:T(8,128)S(1)}, f32[3,64,128]{2,1,0:T(8,128)}, u32[]{:S(2)}) %copy-start.1) | copy-done | bytes 98328
  4.9 0.0 copy-start.2
  4.9 0.8 %copy-done.2 = s32[64,128]{1,0:T(8,128)S(1)} copy-done((s32[64,128]{1,0:T(8,128)S(1)}, s32[64,128]{1,0:T(8,128)}, u32[]{:S(2)}) %copy-start.2) | copy-done | bytes 32792
  5.7 32.4 %shard_map.95 = (f32[4,5,16,8,128]{4,3,2,1,0:T(8,128)S(1)}, f32[4,24,256]{2,1,0:T(8,128)S(1)}) custom-call(f32[3,25]{1,0:T(4,128)S(1)} %constant_dynamic-slice_fusion.refs_0_, f32[25,64,128]{2,1,0:T(8,128)S(1)} %copy-done, f32[3,64,128]{2,1,0:T(8,128)S(1)} %copy-done.1, s32[64,128]{1,0:T(8,128)S(1)} %copy-done.2), custom_call_target="tpu_custom_call" | custom-call | tf_op jit(solution)/shard_map/pallas_call | solution.py:362
  38.1 0.0 copy-done.3
  38.1 12.9 %shard_map.96 = (f32[1600,128]{1,0:T(8,128)S(1)}, f32[64,100]{1,0:T(8,128)S(1)}) custom-call(f32[3,100]{1,0:T(4,128)S(1)} %copy-done.3, f32[112,100]{1,0:T(8,128)S(1)} %pad.8.refs_1_, f32[4,24,256]{2,1,0:T(8,128)S(1)} %get-tuple-element.8.refs_2_, f32[64,2048]{1,0:T(8,128)S(1)} %fusion.refs_3_, f32[4,5,16,8,128]{4,3,2,1,0:T(8,128)S(1)} %get-tuple-element.9.refs_4_), custom_call_target="tpu_custom_call" | custom-call | tf_op jit(solution)/shard_map/pallas_call | solution.py:387
  51.0 0.1 reshape.19
  51.2 14.7 %shard_map.97 = (f32[25,64,128]{2,1,0:T(8,128)S(1)}, f32[8,128]{1,0:T(8,128)S(1)}) custom-call(f32[100,16,128]{2,1,0:T(8,128)S(1)} %bitcast.6, f32[4,64,128]{2,1,0:T(8,128)S(1)} %pad.9.refs_1_), custom_call_target="tpu_custom_call" | custom-call | tf_op jit(solution)/shard_map/pallas_call | solution.py:401
  65.9 0.9 %copy.20 = f32[25,64,128]{2,1,0:T(8,128)} copy(f32[25,64,128]{2,1,0:T(8,128)S(1)} %get-tuple-element.16) | data formatting | bytes 1638400
  66.8 0.6 copy.21
  (4 shorter events, 0.0 us)
Async XLA Ops:
  0.6 37.5 %copy-start.3 = (f32[3,100]{1,0:T(4,128)S(1)}, f32[3,100]{1,0:T(4,128)}, u32[]{:S(2)}) copy-start(f32[3,100]{1,0:T(4,128)} %refs_0_.1) | copy-start | bytes 3604
  0.6 3.4 %copy-start = (f32[25,64,128]{2,1,0:T(8,128)S(1)}, f32[25,64,128]{2,1,0:T(8,128)}, u32[]{:S(2)}) copy-start(f32[25,64,128]{2,1,0:T(8,128)} %refs_1_.1) | copy-start | bytes 2457604
  4.0 0.9 %copy-start.1 = (f32[3,64,128]{2,1,0:T(8,128)S(1)}, f32[3,64,128]{2,1,0:T(8,128)}, u32[]{:S(2)}) copy-start(f32[3,64,128]{2,1,0:T(8,128)} %refs_2_.1) | copy-start | bytes 294916
  4.9 0.8 %copy-start.2 = (s32[64,128]{1,0:T(8,128)S(1)}, s32[64,128]{1,0:T(8,128)}, u32[]{:S(2)}) copy-start(s32[64,128]{1,0:T(8,128)} %refs_3_.1) | copy-start | bytes 98308

commit v5 on v4

--- a/solution.py
+++ b/solution.py
@@ -15,8 +15,6 @@
 VMEM = pl.BlockSpec(memory_space=pltpu.VMEM)
 SMEM = pl.BlockSpec(memory_space=pltpu.SMEM)
 OFF = 4
-PARAMS = pltpu.CompilerParams(vmem_limit_bytes=48 * 1024 * 1024)
-
 
 def remote(number):
     return pltpu.CompilerParams(
@@ -223,54 +221,36 @@
     lax.fori_loop(0, chunks, finish, 0)
 
 
-def result_kernel(local, parts, col_rows, n_tx, n_ty, field_ref, flux_ref, out_ref, sum_ref,
-                  gates, part_flux, tile_flux, *sems):
+def split(x):
+    high = x.astype(jnp.bfloat16)
+    return high, (x - high.astype(jnp.float32)).astype(jnp.bfloat16)
+
+
+def columns_kernel(local, parts, col_rows, n_tx, n_ty, cv_ref, inv_ref, c_ref, m_ref, in_ref,
+                   out_ref, sum_ref, main, side, after, field_ref, got_ref, whole_flux, flux_ref,
+                   gates, part_flux, tile_flux, *sems):
+    levels = local * parts
     me = lax.axis_index("gz")
     tx, ty = lax.axis_index("tx"), lax.axis_index("ty")
-    tile, tiles = tx * n_ty + ty, n_tx * n_ty
+    tile, count = tx * n_ty + ty, n_tx * n_ty
     peers = [lax.rem(me + d, parts) for d in range(1, parts)]
-    others = [lax.rem(tile + d, tiles) for d in range(1, tiles)]
-    rows = lambda at: pl.ds(pl.multiple_of(at * col_rows, col_rows), col_rows)
+    others = [lax.rem(tile + d, count) for d in range(1, count)]
     place = lambda peer: (tx, ty, peer)
     owner = lambda other: (lax.div(other, n_ty), lax.rem(other, n_ty), me)
     gate_rows = lambda at: pl.ds(pl.multiple_of(at * G_DEV, G_DEV), G_DEV)
+    run = 8 * local
+    span = lambda half, at: pl.ds(pl.multiple_of((half * parts + at) * run, 8), run)
     greet([place(p) for p in peers] + [owner(o) for o in others])
 
     def copies(kind, own, peer):
-        levels = pl.ds(peer * local, local)
-        if kind == 0:
-            return send(flux_ref.at[peer], part_flux.at[own], sems[0:2], peer, own, place(peer))
-        if kind == 1:
-            return send(field_ref.at[levels], out_ref.at[:, rows(own), :], sems[2:4], peer, own,
-                        place(peer))
-        return send(gates.at[gate_rows(peer)], tile_flux.at[own], sems[4:6], peer, own, owner(peer))
-
-    for kind in range(2):
-        for peer in peers:
-            copies(kind, me, peer).start()
-    out_ref[:, rows(me), :] = field_ref[pl.ds(me * local, local)]
-    part_flux[me] = flux_ref[me]
-    for peer in peers:
-        copies(0, peer, peer).wait()
-    gates[...] = jnp.sum(part_flux[...], axis=0)
-    for other in others:
-        copies(2, tile, other).start()
-    tile_flux[tile] = gates[gate_rows(tile)]
-    for other in others:
-        copies(2, other, other).wait()
-    sum_ref[...] = jnp.sum(tile_flux[...], axis=0)
-    for peer in peers:
-        copies(1, peer, peer).wait()
-
-
-def split(x):
-    high = x.astype(jnp.bfloat16)
-    return high, (x - high.astype(jnp.float32)).astype(jnp.bfloat16)
-
-
-def columns_kernel(local, parts, col_rows, cv_ref, inv_ref, c_ref, m_ref, in_ref,
-                   out_ref, flux_ref, main, side, after):
-    levels = local * parts
+        if kind == 2:
+            return send(flux_ref.at[peer], part_flux.at[own], sems[4:6], peer, own, place(peer))
+        if kind == 3:
+            return send(gates.at[gate_rows(peer)], tile_flux.at[own], sems[6:8], peer, own,
+                        owner(peer))
+        return send(field_ref.at[span(kind, peer)], got_ref.at[span(kind, own)],
+                    sems[2 * kind : 2 * kind + 2], peer, own, place(peer))
+
     tall = col_rows + 8
     tiles = tall // 8
     lane = lax.broadcasted_iota(jnp.int32, (8, LANES), 1)
@@ -319,23 +299,61 @@
         return carry
 
     lax.fori_loop(0, levels // 4, group, 0)
-    flux = jnp.zeros(flux_ref.shape, jnp.float32)
+    pair = lambda ref, r: jnp.concatenate(
+        [ref[pl.ds(OFF + r + i, levels, stride=tall), :] for i in range(2)], axis=1
+    )
+    slot = lambda r: pl.ds((r // 8) * levels * 8 + r % 8, levels, stride=8)
     for r in range(0, col_rows, 2):
-        ats = [pl.ds(OFF + r + i, levels, stride=tall) for i in range(2)]
         bounds = [c_ref[3, OFF + r + i : OFF + r + i + 1, :LANES] for i in range(2)]
-        field = jnp.concatenate([after[at, :] for at in ats], axis=1)
-        field = solve(field, jnp.concatenate(bounds, axis=1))
+        field = solve(pair(after, r), jnp.concatenate(bounds, axis=1))
         for i in range(2):
-            out_ref[pl.ds(r + i, levels, stride=col_rows), :] = field[:, i * LANES : (i + 1) * LANES]
-        first = jnp.concatenate([main[at, :] for at in ats], axis=1)
+            field_ref[slot(r + i), :] = field[:, i * LANES : (i + 1) * LANES]
+        if r == 6:
+            for peer in peers:
+                copies(0, me, peer).start()
+    flux = jnp.zeros((whole_flux.shape[0], levels), jnp.float32)
+    for r in range(0, col_rows, 2):
+        second = jnp.concatenate([field_ref[slot(r + i), :] for i in range(2)], axis=1)
         cells = split(m_ref[:, r * LANES : (r + 2) * LANES])
-        total = split(field + first)
+        total = split(second + pair(main, r))
         for one, two in ((0, 0), (0, 1), (1, 0)):
             flux += lax.dot_general(
                 cells[one], total[two], (((1,), (1,)), ((), ())),
                 preferred_element_type=jnp.float32,
             )
-    flux_ref[...] = flux
+    whole_flux[...] = jnp.zeros(whole_flux.shape, jnp.float32)
+    whole_flux[:, :levels] = flux
+    for part in range(parts):
+        shift = (LANES - part * local) % LANES
+        shifted = whole_flux[...]
+        flux_ref[part] = pltpu.roll(shifted, shift, 1) if shift else shifted
+    for kind in (2, 1):
+        for peer in peers:
+            copies(kind, me, peer).start()
+    part_flux[me] = flux_ref[me]
+    for peer in peers:
+        copies(2, peer, peer).wait()
+    gates[...] = jnp.sum(part_flux[...], axis=0)
+    for other in others:
+        copies(3, tile, other).start()
+    tile_flux[tile] = gates[gate_rows(tile)]
+    for half in range(2):
+        got_ref[span(half, me), :] = field_ref[span(half, me), :]
+        for peer in peers:
+            copies(half, peer, peer).wait()
+
+    def place_level(l, carry):
+        for part in range(parts):
+            for half in range(2):
+                row = pl.multiple_of((half * parts + part) * run + 8 * l, 8)
+                start = part * col_rows + 8 * half
+                out_ref[l, start : start + 8, :] = got_ref[pl.ds(row, 8), :]
+        return carry
+
+    lax.fori_loop(0, local, place_level, 0)
+    for other in others:
+        copies(3, other, other).wait()
+    sum_ref[...] = jnp.sum(tile_flux[...], axis=0)
 
 
 def per_device(tracer_in, coef_h, coef_v, wet_levels, column_inv, sec_cell, sec_gate, sec_weight):
@@ -384,39 +402,30 @@
         compiler_params=remote(0),
     )(coef_depth, tracer_in, coef_h, wet_levels)
 
-    field, flux = pl.pallas_call(
-        lambda *refs: columns_kernel(local_levels, depth_count, col_rows, *refs),
-        out_shape=(
-            jax.ShapeDtypeStruct((levels * col_rows, LANES), jnp.float32),
-            jax.ShapeDtypeStruct((G_DEV * tiles, levels), jnp.float32),
-        ),
-        in_specs=[SMEM, VMEM, VMEM, VMEM, VMEM],
-        out_specs=(VMEM, VMEM),
-        scratch_shapes=[pltpu.VMEM((levels * tall, LANES), jnp.float32)] * 3,
-        compiler_params=PARAMS,
-    )(coef_v, jnp.pad(column_inv.T, ((0, -levels % 16), (0, 0))), window, gate_cells, got)
-    field = field.reshape(levels, col_rows, width)
-    flux = flux.reshape(-1, depth_count, local_levels).transpose(1, 0, 2)
-    flux = jnp.pad(flux, ((0, 0), (0, 0), (0, LANES - local_levels)))
+    gates = G_DEV * tiles
     out, flux = pl.pallas_call(
-        lambda *refs: result_kernel(
+        lambda *refs: columns_kernel(
             local_levels, depth_count, col_rows, lax.axis_size("tx"), lax.axis_size("ty"), *refs
         ),
         out_shape=(
             jax.ShapeDtypeStruct((local_levels, rows, width), jnp.float32),
             jax.ShapeDtypeStruct((G_DEV, LANES), jnp.float32),
         ),
-        in_specs=[VMEM, VMEM],
+        in_specs=[SMEM, VMEM, VMEM, VMEM, VMEM],
         out_specs=(VMEM, VMEM),
-        scratch_shapes=[
-            pltpu.VMEM((G_DEV * tiles, LANES), jnp.float32),
-            pltpu.VMEM((depth_count, G_DEV * tiles, LANES), jnp.float32),
+        scratch_shapes=[pltpu.VMEM((levels * tall, LANES), jnp.float32)] * 3
+        + [pltpu.VMEM((levels * col_rows, LANES), jnp.float32)] * 2
+        + [
+            pltpu.VMEM((gates, LANES), jnp.float32),
+            pltpu.VMEM((depth_count, gates, LANES), jnp.float32),
+            pltpu.VMEM((gates, LANES), jnp.float32),
+            pltpu.VMEM((depth_count, gates, LANES), jnp.float32),
             pltpu.VMEM((tiles, G_DEV, LANES), jnp.float32),
         ]
-        + [dma((depth_count,))] * 4
+        + [dma((depth_count,))] * 6
         + [dma((tiles,))] * 2,
         compiler_params=remote(1),
-    )(field, flux)
+    )(coef_v, jnp.pad(column_inv.T, ((0, -levels % 16), (0, 0))), window, gate_cells, got)
     flux = flux[:, :local_levels]
     return (out, flux)
 

time: 67.7 us -> 67 us (0.990)
    pallas_call x1 -> x0, Pallas kernels: 14.7 us -> none  [per_device(): pl.pallas_call(lambda *refs: result_kernel(local_levels, depth_count, col...]
    pallas_call x1, Pallas kernels: 12.9 us -> 27.1 us  [per_device(): pl.pallas_call(lambda *refs: columns_kernel(local_levels, depth_count, co...]
where the time goes in v5:
time: 67 us; the launch traced here: 66.7 us
  Pallas kernels  59.5 us (89%)
  local copies, waits for them, and re-layouts  4.88 us (7%)
  matrix products  1.62 us (2%)
  between operations  0.7 us (1%)
    pallas_call x1, Pallas kernels, per_device(): pl.pallas_call(lambda *refs: levels_kernel(local_levels, depth_count, col...  32.4 us
    pallas_call x1, Pallas kernels, per_device(): pl.pallas_call(lambda *refs: columns_kernel(local_levels, depth_count, co...  27.1 us
    unnamed x11, local copies, waits for them, and re-layouts  4.04 us
    dot_general x1, matrix products, per_device(): gate_cells = jnp.dot(gate_hot, cell_hot, precision=HI)  1.62 us

profile of v5, /device:TPU:1, one launch (start us, length us, event | category | flops | bytes accessed | tf_op | source)
XLA Modules:
  0.0 66.7 jit_solution(14461915884766144763)
XLA Ops:
  0.6 0.0 copy-start.3
  0.6 0.0 copy-start
  0.7 0.8 %constant_dynamic-slice_fusion.refs_0_ = f32[3,25]{1,0:T(4,128)S(1)} fusion(f32[3,100]{1,0:T(4,128)} %refs_0_.1, s32[]{:T(128)S(6)} %select_n.7), kind=kLoop, calls=%fused_computation.10 | loop fusion | bytes 604 | tf_op jit(solution)/shard_map/dynamic_slice | solution.py:368
  1.5 0.9 %copy.10 = f32[100,100]{0,1:T(8,128)S(1)} copy(f32[100,100]{1,0:T(8,128)} %param.12) | data formatting | bytes 80000 | tf_op args[4]
  2.4 1.6 %fusion.refs_3_ = f32[64,2048]{1,0:T(8,128)S(1)} fusion(s32[2048]{0:T(1024)S(1)} %iota_add_fusion, s32[256]{0:T(256)} %param.13, f32[256]{0:T(256)} %param.15, s32[256]{0:T(256)} %param.14), kind=kOutput, calls=%fused_computation | convolution fusion | flops 403210240 | bytes 535552 | tf_op jit(solution)/shard_map/dot_general | solution.py:375
  4.0 0.0 copy-done
  4.0 0.0 copy-start.1
  4.1 0.9 %copy-done.1 = f32[3,64,128]{2,1,0:T(8,128)S(1)} copy-done((f32[3,64,128]{2,1,0:T(8,128)S(1)}, f32[3,64,128]{2,1,0:T(8,128)}, u32[]{:S(2)}) %copy-start.1) | copy-done | bytes 98328
  4.9 0.0 copy-start.2
  4.9 0.8 %copy-done.2 = s32[64,128]{1,0:T(8,128)S(1)} copy-done((s32[64,128]{1,0:T(8,128)S(1)}, s32[64,128]{1,0:T(8,128)}, u32[]{:S(2)}) %copy-start.2) | copy-done | bytes 32792
  5.7 32.4 %shard_map.95 = (f32[4,5,16,8,128]{4,3,2,1,0:T(8,128)S(1)}, f32[4,24,256]{2,1,0:T(8,128)S(1)}) custom-call(f32[3,25]{1,0:T(4,128)S(1)} %constant_dynamic-slice_fusion.refs_0_, f32[25,64,128]{2,1,0:T(8,128)S(1)} %copy-done, f32[3,64,128]{2,1,0:T(8,128)S(1)} %copy-done.1, s32[64,128]{1,0:T(8,128)S(1)} %copy-done.2), custom_call_target="tpu_custom_call" | custom-call | tf_op jit(solution)/shard_map/pallas_call | solution.py:380
  38.1 0.0 copy-done.3
  38.1 27.1 %shard_map.96 = (f32[25,64,128]{2,1,0:T(8,128)S(1)}, f32[8,128]{1,0:T(8,128)S(1)}) custom-call(f32[3,100]{1,0:T(4,128)S(1)} %copy-done.3, f32[112,100]{1,0:T(8,128)S(1)} %pad.4.refs_1_, f32[4,24,256]{2,1,0:T(8,128)S(1)} %get-tuple-element.6.refs_2_, f32[64,2048]{1,0:T(8,128)S(1)} %fusion.refs_3_, f32[4,5,16,8,128]{4,3,2,1,0:T(8,128)S(1)} %get-tuple-element.7.refs_4_), custom_call_target="tpu_custom_call" | custom-call | tf_op jit(solution)/shard_map/pallas_call | solution.py:406
  65.2 0.9 %copy.13 = f32[25,64,128]{2,1,0:T(8,128)} copy(f32[25,64,128]{2,1,0:T(8,128)S(1)} %get-tuple-element.12) | data formatting | bytes 1638400
  66.1 0.6 copy.14
  (2 shorter events, 0.0 us)
Async XLA Ops:
  0.6 37.5 %copy-start.3 = (f32[3,100]{1,0:T(4,128)S(1)}, f32[3,100]{1,0:T(4,128)}, u32[]{:S(2)}) copy-start(f32[3,100]{1,0:T(4,128)} %refs_0_.1) | copy-start | bytes 3604
  0.6 3.4 %copy-start = (f32[25,64,128]{2,1,0:T(8,128)S(1)}, f32[25,64,128]{2,1,0:T(8,128)}, u32[]{:S(2)}) copy-start(f32[25,64,128]{2,1,0:T(8,128)} %refs_1_.1) | copy-start | bytes 2457604
  4.0 0.9 %copy-start.1 = (f32[3,64,128]{2,1,0:T(8,128)S(1)}, f32[3,64,128]{2,1,0:T(8,128)}, u32[]{:S(2)}) copy-start(f32[3,64,128]{2,1,0:T(8,128)} %refs_2_.1) | copy-start | bytes 294916
  4.9 0.8 %copy-start.2 = (s32[64,128]{1,0:T(8,128)S(1)}, s32[64,128]{1,0:T(8,128)}, u32[]{:S(2)}) copy-start(s32[64,128]{1,0:T(8,128)} %refs_3_.1) | copy-start | bytes 98308

commit v6 on v5

--- a/solution.py
+++ b/solution.py
@@ -62,7 +62,7 @@
         p_ref[l, :rows, :LANES] = tracer_ref[l]
         return carry
 
-    lax.fori_loop(0, local, fill, 0)
+    lax.fori_loop(0, local, fill, 0, unroll=5)
     for c in range(3):
         p_ref[local + c, :rows, :LANES] = coef_ref[c]
     p_ref[local + 3, :rows, :LANES] = wet_ref[...].astype(jnp.float32)
@@ -113,7 +113,7 @@
         x_sent[1, q] = west
         return carry
 
-    lax.fori_loop(0, pairs, pack, 0)
+    lax.fori_loop(0, pairs, pack, 0, unroll=3)
     start(0)
 
     @pl.when(jnp.logical_not(has_prior[0]))
@@ -146,7 +146,7 @@
                 p_ref[2 * q + j, 8 * t : 8 * t + 8, LANES:] = tile
         return carry
 
-    lax.fori_loop(0, pairs, unpack, 0)
+    lax.fori_loop(0, pairs, unpack, 0, unroll=3)
     start(2)
     wait(1)
     wait(2)
@@ -174,7 +174,7 @@
             k = (me * local + l).astype(jnp.float32)
             wet = jnp.where(k < p_ref[local + 3], 1.0, 0.0)
             a = wet * p_ref[l]
-            a = substeps(a, wet, *(c[...] * cv_ref[i, l] for i, c in enumerate(coefs)))
+            a = substeps(a, wet, *(c[...] * cv_ref[i, me * local + l] for i, c in enumerate(coefs)))
             a = pltpu.roll(a, OFF, 0)
             for part in range(parts):
                 for t in range(tiles):
@@ -365,7 +365,6 @@
     col_rows = rows // depth_count
     tall = col_rows + 8
     chunks = local_levels // 5
-    coef_depth = lax.dynamic_slice_in_dim(coef_v, depth_index * local_levels, local_levels, 1)
     row_start = depth_index * col_rows
 
     gate_ids = jnp.arange(G_DEV * tiles, dtype=jnp.int32)
@@ -400,7 +399,7 @@
             dma((depth_count, chunks)),
         ],
         compiler_params=remote(0),
-    )(coef_depth, tracer_in, coef_h, wet_levels)
+    )(coef_v, tracer_in, coef_h, wet_levels)
 
     gates = G_DEV * tiles
     out, flux = pl.pallas_call(

time: 67 us -> 65.4 us (0.976)
  Pallas kernels: 59.5 us -> 58 us
    pallas_call x1, Pallas kernels: 32.4 us -> 30.9 us  [per_device(): pl.pallas_call(lambda *refs: levels_kernel(local_levels, depth_count, col...]
    dynamic_slice x1 -> x0, local copies, waits for them, and re-layouts: 0.83 us -> none  [per_device(): lax.dynamic_slice_in_dim(coef_v, depth_index * local_levels, local_levels...]
    unnamed x11, local copies, waits for them, and re-layouts: 4.04 us -> 4.79 us
where the time goes in v6:
time: 65.4 us; the launch traced here: 65.1 us
  Pallas kernels  58 us (89%)
  local copies, waits for them, and re-layouts  4.8 us (7%)
  matrix products  1.62 us (2%)
  between operations  0.69 us (1%)
    pallas_call x1, Pallas kernels, per_device(): pl.pallas_call(lambda *refs: levels_kernel(local_levels, depth_count, col...  30.9 us
    pallas_call x1, Pallas kernels, per_device(): pl.pallas_call(lambda *refs: columns_kernel(local_levels, depth_count, co...  27.1 us
    unnamed x11, local copies, waits for them, and re-layouts  4.79 us
    dot_general x1, matrix products, per_device(): gate_cells = jnp.dot(gate_hot, cell_hot, precision=HI)  1.62 us

profile of v6, /device:TPU:1, one launch (start us, length us, event | category | flops | bytes accessed | tf_op | source)
XLA Modules:
  0.0 65.1 jit_solution(2362971087450058008)
XLA Ops:
  0.6 0.0 copy-start
  0.7 1.0 %copy.10 = f32[100,100]{0,1:T(8,128)S(1)} copy(f32[100,100]{1,0:T(8,128)} %param.12) | data formatting | bytes 80000 | tf_op args[4]
  1.6 1.6 %fusion.refs_3_ = f32[64,2048]{1,0:T(8,128)S(1)} fusion(s32[2048]{0:T(1024)S(1)} %iota_add_fusion, s32[256]{0:T(256)} %param.13, f32[256]{0:T(256)} %param.15, s32[256]{0:T(256)} %param.14), kind=kOutput, calls=%fused_computation | convolution fusion | flops 403210240 | bytes 535552 | tf_op jit(solution)/shard_map/dot_general | solution.py:374
  3.3 0.0 copy-done
  3.3 0.0 copy-start.1
  3.3 0.9 %copy-done.1 = f32[3,64,128]{2,1,0:T(8,128)S(1)} copy-done((f32[3,64,128]{2,1,0:T(8,128)S(1)}, f32[3,64,128]{2,1,0:T(8,128)}, u32[]{:S(2)}) %copy-start.1) | copy-done | bytes 98328
  4.2 0.0 copy-start.2
  4.2 0.8 %copy-done.2 = s32[64,128]{1,0:T(8,128)S(1)} copy-done((s32[64,128]{1,0:T(8,128)S(1)}, s32[64,128]{1,0:T(8,128)}, u32[]{:S(2)}) %copy-start.2) | copy-done | bytes 32792
  4.9 0.0 copy-start.3
  4.9 0.7 %copy-done.3 = f32[3,100]{1,0:T(4,128)S(1)} copy-done((f32[3,100]{1,0:T(4,128)S(1)}, f32[3,100]{1,0:T(4,128)}, u32[]{:S(2)}) %copy-start.3) | copy-done | bytes 1224
  5.6 30.9 %shard_map.95 = (f32[4,5,16,8,128]{4,3,2,1,0:T(8,128)S(1)}, f32[4,24,256]{2,1,0:T(8,128)S(1)}) custom-call(f32[3,100]{1,0:T(4,128)S(1)} %copy-done.3, f32[25,64,128]{2,1,0:T(8,128)S(1)} %copy-done, f32[3,64,128]{2,1,0:T(8,128)S(1)} %copy-done.1, s32[64,128]{1,0:T(8,128)S(1)} %copy-done.2), custom_call_target="tpu_custom_call" | custom-call | tf_op jit(solution)/shard_map/pallas_call | solution.py:379
  36.6 27.1 %shard_map.96 = (f32[25,64,128]{2,1,0:T(8,128)S(1)}, f32[8,128]{1,0:T(8,128)S(1)}) custom-call(f32[3,100]{1,0:T(4,128)S(1)} %copy-done.3, f32[112,100]{1,0:T(8,128)S(1)} %pad.4.refs_1_, f32[4,24,256]{2,1,0:T(8,128)S(1)} %get-tuple-element.6.refs_2_, f32[64,2048]{1,0:T(8,128)S(1)} %fusion.refs_3_, f32[4,5,16,8,128]{4,3,2,1,0:T(8,128)S(1)} %get-tuple-element.7.refs_4_), custom_call_target="tpu_custom_call" | custom-call | tf_op jit(solution)/shard_map/pallas_call | solution.py:405
  63.6 0.9 %copy.13 = f32[25,64,128]{2,1,0:T(8,128)} copy(f32[25,64,128]{2,1,0:T(8,128)S(1)} %get-tuple-element.12) | data formatting | bytes 1638400
  64.5 0.6 copy.14
  (2 shorter events, 0.0 us)
Async XLA Ops:
  0.6 2.6 %copy-start = (f32[25,64,128]{2,1,0:T(8,128)S(1)}, f32[25,64,128]{2,1,0:T(8,128)}, u32[]{:S(2)}) copy-start(f32[25,64,128]{2,1,0:T(8,128)} %refs_1_.1) | copy-start | bytes 2457604
  3.3 0.9 %copy-start.1 = (f32[3,64,128]{2,1,0:T(8,128)S(1)}, f32[3,64,128]{2,1,0:T(8,128)}, u32[]{:S(2)}) copy-start(f32[3,64,128]{2,1,0:T(8,128)} %refs_2_.1) | copy-start | bytes 294916
  4.2 0.8 %copy-start.2 = (s32[64,128]{1,0:T(8,128)S(1)}, s32[64,128]{1,0:T(8,128)}, u32[]{:S(2)}) copy-start(s32[64,128]{1,0:T(8,128)} %refs_3_.1) | copy-start | bytes 98308
  4.9 0.7 %copy-start.3 = (f32[3,100]{1,0:T(4,128)S(1)}, f32[3,100]{1,0:T(4,128)}, u32[]{:S(2)}) copy-start(f32[3,100]{1,0:T(4,128)} %refs_0_.3) | copy-start | bytes 3604
